TPU v7x, 32 devices: a whole 2x2x4 slice. The times are simulated.
32 devices in a mesh: slide: 2 (over y), row: 4 (over z), col: 4 (over x, core).
Axes of the slice: x: 2, y: 2, z: 4, core: 2. Of those that a mesh axis runs over, the one named last changes fastest.
Arguments:
- tokens: bfloat16 [256, 256, 512], P(('slide', 'row'), 'col'), parts along dimension 0, may hold values from -6 to 6
- tissue_list: int32 [8, 4, 24], P('slide'), parts along dimension 0, may hold values from -1 to 31, as said below
- ln_gain: float32 [512], replicated, may hold values from 0.1 to 1.9
- w_qkv: bfloat16 [512, 1536], replicated, may hold values from -16 to 16
- w_out: bfloat16 [512, 512], replicated, may hold values from -2 to 2
- conv_weight: float32 [7, 7, 512], replicated, may hold values from -0.875 to 0.875
- conv_bias: float32 [512], replicated, may hold values from -4 to 4
- conv_gain: float32 [512], replicated, may hold values from 0.1 to 1.9
Outputs:
- encoded: bfloat16 [256, 256, 512], P(('slide', 'row'), 'col'), parts along dimension 0
There are 2 independent parts, one for each index of `slide`. A program takes and returns all parts, laid end to end along the dimension named above; an argument that names none is the same for every part. Nothing has to cross between parts.
Inputs may be any that keep to these rules, and one draw needn't show every extreme that they name: `tissue_list`: each tile's list holds distinct local block numbers (block row * 8 + block column) first, then -1 entries; it names at least one block, and some tile names 24 blocks.
All inputs are finite; a program needn't handle non-finite values.
Results may differ from a plain program's by a relative error of at most 0.0063.
Values may be sent and summed in bfloat16 or wider, within the bound.
A program may use at most 128 MiB of HBM per device.

v0:
```python
import jax
import jax.numpy as jnp
from jax import lax
from jax.sharding import PartitionSpec as P

HEADS = 8
BLK = 8
BR = 4
BC = 8


def with_halo(shard, sides, width):
    for axis, dim in sides:
        devices, length = (lax.axis_size(axis), shard.shape[dim])
        up = [(i, (i + 1) % devices) for i in range(devices - 1)]
        down = [(j, i) for i, j in up]
        last = lax.slice_in_dim(shard, length - width, length, axis=dim)
        initial = lax.slice_in_dim(shard, 0, width, axis=dim)
        before = lax.ppermute(last, axis, up)
        after = lax.ppermute(initial, axis, down)
        shard = jnp.concatenate([before, shard, after], axis=dim)
    return shard


def layer_norm(values, gain):
    mean = jnp.mean(values, axis=-1, keepdims=True)
    centred = values - mean
    variance = jnp.mean(centred * centred, axis=-1, keepdims=True)
    return centred * lax.rsqrt(variance + 1e-06) * gain


def block_table(tissue_list):
    tiles_r, tiles_c, slots = tissue_list.shape
    hits = jnp.any(tissue_list[..., None] == jnp.arange(BR * BC, dtype=jnp.int32), axis=2)
    hits = hits.reshape(tiles_r, tiles_c, BR, BC).transpose(0, 2, 1, 3)
    return hits.reshape(tiles_r * BR, tiles_c * BC)


def attend(query, keys, values, key_ok):
    rows = query.shape[0]
    span = keys.shape[0]
    head_dim = query.shape[1] // HEADS
    qh = query.reshape(rows, HEADS, head_dim)
    kh = keys.reshape(span, HEADS, head_dim)
    vh = values.reshape(span, HEADS, head_dim)
    scores = jnp.einsum("rhd,shd->hrs", qh, kh, preferred_element_type=jnp.float32) * head_dim ** (
        -0.5
    )
    scores = jnp.where(key_ok[None, None, :], scores, -1e30)
    top = jnp.max(scores, axis=-1, keepdims=True)
    weights = jnp.exp(scores - top)
    probs = (weights / jnp.sum(weights, axis=-1, keepdims=True)).astype(jnp.bfloat16)
    out = jnp.einsum("hrs,shd->rhd", probs, vh, preferred_element_type=jnp.float32)
    return out.reshape(rows, HEADS * head_dim).astype(jnp.bfloat16)


def per_device(tokens, tissue_list, ln_gain, w_qkv, w_out, conv_weight, conv_bias, conv_gain):
    tile_h, tile_w, width = tokens.shape
    token_count = BLK * BLK
    anchor = jnp.zeros((), jnp.int32)
    normed = layer_norm(tokens.astype(jnp.float32), ln_gain).astype(jnp.bfloat16)
    flat_normed = normed.reshape(-1, width)
    projected = jnp.dot(flat_normed, w_qkv, preferred_element_type=jnp.float32)
    projected = projected.astype(jnp.bfloat16).reshape(tile_h, tile_w, 3 * width)
    query = projected[..., :width]
    pairs = with_halo(projected[..., width:], (("row", 0), ("col", 1)), BLK)
    pair_blocks = pairs.reshape(BR + 2, BLK, BC + 2, BLK, 2 * width).transpose(0, 2, 1, 3, 4)
    pair_blocks = pair_blocks.reshape(BR + 2, BC + 2, token_count, 2 * width)
    query_blocks = query.reshape(BR, BLK, BC, BLK, width).transpose(0, 2, 1, 3, 4)
    query_blocks = query_blocks.reshape(BR, BC, token_count, width)
    table = jnp.pad(block_table(tissue_list), 1)
    row_index = lax.axis_index("row")
    col_index = lax.axis_index("col")
    near_table = lax.dynamic_slice(table, (row_index * BR, col_index * BC), (BR + 2, BC + 2))
    own_table = near_table[1:-1, 1:-1]

    def finish(query_block, window, key_ok):
        out = attend(query_block, window[:, :width], window[:, width:], key_ok)
        return jnp.dot(out, w_out, preferred_element_type=jnp.float32)

    def block_row(bi):
        near = lax.dynamic_slice(
            pair_blocks, (bi, anchor, anchor, anchor), (3, BC + 2, token_count, 2 * width)
        )
        near_ok = lax.dynamic_slice(near_table, (bi, anchor), (3, BC + 2))
        window = jnp.stack([near[:, b : b + BC] for b in range(3)], axis=1)
        window = window.transpose(2, 0, 1, 3, 4).reshape(BC, 9 * token_count, 2 * width)
        okay = jnp.stack([near_ok[:, b : b + BC] for b in range(3)], axis=1)
        okay = jnp.repeat(okay.transpose(2, 0, 1).reshape(BC, 9), token_count, axis=1)
        row_queries = lax.dynamic_slice(
            query_blocks, (bi, anchor, anchor, anchor), (1, BC, token_count, width)
        )[0]
        return jax.vmap(finish)(row_queries, window, okay)

    deltas = lax.map(block_row, jnp.arange(BR, dtype=jnp.int32))
    deltas = jnp.where(own_table[:, :, None, None], deltas, 0.0)
    deltas = (
        deltas.reshape(BR, BC, BLK, BLK, width)
        .transpose(0, 2, 1, 3, 4)
        .reshape(tile_h, tile_w, width)
    )
    mixed = (tokens.astype(jnp.float32) + deltas).astype(jnp.bfloat16)
    framed = with_halo(mixed, (("row", 0), ("col", 1)), 3)
    filtered = jnp.zeros((tile_h, tile_w, width), jnp.float32)
    for dy in range(7):
        for dx in range(7):
            filtered = (
                filtered
                + framed[dy : dy + tile_h, dx : dx + tile_w].astype(jnp.float32)
                * conv_weight[dy, dx]
            )
    filtered = filtered + conv_bias
    branch = layer_norm(filtered, conv_gain)
    return (mixed.astype(jnp.float32) + branch).astype(jnp.bfloat16)


def solution(mesh):
    in_specs = (
        P(("slide", "row"), "col", None),
        P("slide", None, None),
        P(),
        P(),
        P(),
        P(),
        P(),
        P(),
    )
    out_specs = P(("slide", "row"), "col", None)
    return jax.shard_map(
        per_device, mesh=mesh, in_specs=in_specs, out_specs=out_specs, check_vma=False
    )
```

profile of v0, /device:TPU:1, one launch (start us, length us, event | category | flops | bytes accessed | tf_op | source)
XLA Modules:
  0.0 460.0 jit_solution(1990288445605845165)
XLA Ops:
  9.5 4.1 collective-permute-start
  15.4 19.9 %collective-permute-done = bf16[8,64,1024]{2,1,0:T(8,128)(2,1)S(1)} collective-permute-done((bf16[8,64,1024]{2,1,0:T(8,128)(2,1)S(1)}, bf16[8,64,1024]{2,1,0:T(8,128)(2,1)S(1)}, u32[]{:S(2)}, u32[]{:S(2)}) %collective-permute-start) | collective-permute-done | bytes 1048608 | tf_op jit(solution)/shard_map/ppermute | solution.py:19
  35.3 3.9 collective-permute-done.1
  40.4 4.9 %collective-permute-start.2 = (bf16[48,8,1024]{2,1,0:T(8,128)(2,1)}, bf16[48,8,1024]{2,1,0:T(8,128)(2,1)S(1)}, u32[]{:S(2)}, u32[]{:S(2)}) collective-permute-start(bf16[48,8,1024]{2,1,0:T(8,128)(2,1)} %get-tuple-element.92), channel_id=1, source_target_pairs={{0,1},{1,2},{2,3},{4,5},{5,6},{6,7},{8,9},{9,10},{10,11},{12,13},{... | collective-permute-start | bytes 2359304 | tf_op jit(solution)/shard_map/ppermute | solution.py:19
  58.7 4.1 pad_maximum_fusion.1
  62.8 4.1 copy.67
  66.9 325.6 %while.11 = (s32[]{:T(128)}, f32[4,8,64,512]{3,2,1,0:T(8,128)}, s32[4]{0:T(128)S(1)}, bf16[6,10,64,1024]{3,2,1,0:T(8,128)(2,1)}, pred[6,10]{1,0:T(8,128)(4,1)}, ...) while((s32[]{:T(128)}, f32[4,8,64,512]{3,2,1,0:T(8,128)}, s32[4]{0:T(128)S(1)}, ...), condition=%wide.region_6.7_spmd.clone, body=%wide.region_3.6_spmd.sunk.clone | while | flops 900989632 | bytes 148950448 | solution.py:95
  69.4 5.9 %constant_dynamic-slice_fusion.11 = (bf16[3,8,64,1024]{3,2,1,0:T(8,128)(2,1)S(1)}, bf16[3,8,64,1024]{3,2,1,0:T(8,128)(2,1)S(1)}, bf16[3,8,64,1024]{3,2,1,0:T(8,128)(2,1)S(1)}) fusion(bf16[6,10,64,1024]{3,2,1,0:T(8,128)(2,1)} %get-tuple-element.268, s32[]{:T(128)S(6)} %select_n.42, s32[]{:T(128)S(6)} %add.1074, s32[]{:T(128)S(6)} %add.1075), kind=kLoop, calls=%fused_computation.24.clone.1.clone | loop fusion | bytes 18874380 | tf_op jit(solution)/shard_map/while/body/eval_jaxpr/slice | solution.py:86
  75.3 3.9 copy_bitcast_fusion.7
  81.3 8.4 %pad_maximum_fusion.13 = bf16[3,3,8,64,1024]{4,3,1,0,2:T(8,128)(2,1)} fusion(bf16[3,1,8,64,1024]{4,3,1,0,2:T(8,128)(2,1)} %get-tuple-element.228, bf16[3,1,8,64,1024]{4,3,1,0,2:T(8,128)(2,1)} %get-tuple-element.229, bf16[3,1,8,64,1024]{4,3,1,0,2:T(8,128)(2,1)} %bitcast.156), kind=kLoop, calls=%fused_computation.4.clone.1.clone | loop fusion | flops 9437184 | bytes 18874368 | tf_op jit(solution)/shard_map/while/body/eval_jaxpr/stack | solution.py:86
  89.7 8.3 %fusion.90 = (bf16[8,576,512]{2,1,0:T(8,128)(2,1)}, bf16[8,576,512]{2,1,0:T(8,128)(2,1)}) fusion(bf16[8,576,1024]{2,1,0:T(8,128)(2,1)} %bitcast.153), kind=kLoop, calls=%fused_computation.104.clone.1.clone | loop fusion | bytes 18874368 | tf_op jit(solution)/shard_map/while/body/eval_jaxpr/vmap()/slice | solution.py:78
  98.0 7.7 %copy.85 = bf16[8,576,512]{1,2,0:T(8,128)(2,1)} copy(bf16[8,576,512]{2,1,0:T(8,128)(2,1)} %get-tuple-element.232) | data formatting | bytes 9437184 | tf_op jit(solution)/shard_map/while/body/eval_jaxpr/vmap()/slice | solution.py:78
  108.6 7.9 %fusion.91 = f32[8,8,64,576]{3,2,1,0:T(8,128)} fusion(bf16[8,576,8,64]{1,3,2,0:T(8,128)(2,1)} %bitcast.154, bf16[8,64,8,64]{3,2,1,0:T(8,128)(2,1)S(1)} %squeeze.9), kind=kOutput, calls=%fused_computation.16.clone.1.clone | convolution fusion | flops 301989888 | bytes 14680064 | tf_op jit(solution)/shard_map/while/body/eval_jaxpr/vmap(rhd,shd->hrs)/dot_general | solution.py:46
  117.6 14.1 %fusion.92 = (f32[8,8,64]{2,1,0:T(8,128)S(1)}, f32[8,8,64,576]{3,2,1,0:T(8,128)}) fusion(f32[8,8,64,576]{3,2,1,0:T(8,128)} %fusion.91, pred[8,576]{1,0:T(8,128)(4,1)S(1)} %broadcast_in_dim.75), kind=kOutput, calls=%fused_computation.105.clone.1.clone | output fusion | flops 14156351 | bytes 18895360 | tf_op jit(solution)/shard_map/while/body/eval_jaxpr/vmap()/sub | solution.py:51
  131.7 7.7 %copy.84 = bf16[8,576,512]{1,2,0:T(8,128)(2,1)} copy(bf16[8,576,512]{2,1,0:T(8,128)(2,1)} %get-tuple-element.231) | data formatting | bytes 9437184 | tf_op jit(solution)/shard_map/while/body/eval_jaxpr/vmap()/slice | solution.py:78
  139.4 7.4 %fusion.93 = bf16[8,8,64,64]{3,2,1,0:T(8,128)(2,1)S(1)} fusion(bf16[8,576,8,64]{1,3,2,0:T(8,128)(2,1)} %bitcast.157, f32[8,8,64,576]{3,2,1,0:T(8,128)} %get-tuple-element.236, f32[8,8,64]{2,1,0:T(8,128)S(1)} %get-tuple-element.237), kind=kOutput, calls=%fused_computation.13.clone.1.clone | convolution fusion | flops 306970624 | bytes 14696448 | tf_op jit(solution)/shard_map/while/body/eval_jaxpr/vmap(hrs,shd->rhd)/dot_general | solution.py:53
  150.8 5.8 %constant_dynamic-slice_fusion.11 = (bf16[3,8,64,1024]{3,2,1,0:T(8,128)(2,1)S(1)}, bf16[3,8,64,1024]{3,2,1,0:T(8,128)(2,1)S(1)}, bf16[3,8,64,1024]{3,2,1,0:T(8,128)(2,1)S(1)}) fusion(bf16[6,10,64,1024]{3,2,1,0:T(8,128)(2,1)} %get-tuple-element.268, s32[]{:T(128)S(6)} %select_n.42, s32[]{:T(128)S(6)} %add.1074, s32[]{:T(128)S(6)} %add.1075), kind=kLoop, calls=%fused_computation.24.clone.1.clone | loop fusion | bytes 18874380 | tf_op jit(solution)/shard_map/while/body/eval_jaxpr/slice | solution.py:86
  156.6 3.9 copy_bitcast_fusion.7
  162.7 8.4 %pad_maximum_fusion.13 = bf16[3,3,8,64,1024]{4,3,1,0,2:T(8,128)(2,1)} fusion(bf16[3,1,8,64,1024]{4,3,1,0,2:T(8,128)(2,1)} %get-tuple-element.228, bf16[3,1,8,64,1024]{4,3,1,0,2:T(8,128)(2,1)} %get-tuple-element.229, bf16[3,1,8,64,1024]{4,3,1,0,2:T(8,128)(2,1)} %bitcast.156), kind=kLoop, calls=%fused_computation.4.clone.1.clone | loop fusion | flops 9437184 | bytes 18874368 | tf_op jit(solution)/shard_map/while/body/eval_jaxpr/stack | solution.py:86
  171.1 8.3 %fusion.90 = (bf16[8,576,512]{2,1,0:T(8,128)(2,1)}, bf16[8,576,512]{2,1,0:T(8,128)(2,1)}) fusion(bf16[8,576,1024]{2,1,0:T(8,128)(2,1)} %bitcast.153), kind=kLoop, calls=%fused_computation.104.clone.1.clone | loop fusion | bytes 18874368 | tf_op jit(solution)/shard_map/while/body/eval_jaxpr/vmap()/slice | solution.py:78
  179.4 7.7 %copy.85 = bf16[8,576,512]{1,2,0:T(8,128)(2,1)} copy(bf16[8,576,512]{2,1,0:T(8,128)(2,1)} %get-tuple-element.232) | data formatting | bytes 9437184 | tf_op jit(solution)/shard_map/while/body/eval_jaxpr/vmap()/slice | solution.py:78
  190.0 7.9 %fusion.91 = f32[8,8,64,576]{3,2,1,0:T(8,128)} fusion(bf16[8,576,8,64]{1,3,2,0:T(8,128)(2,1)} %bitcast.154, bf16[8,64,8,64]{3,2,1,0:T(8,128)(2,1)S(1)} %squeeze.9), kind=kOutput, calls=%fused_computation.16.clone.1.clone | convolution fusion | flops 301989888 | bytes 14680064 | tf_op jit(solution)/shard_map/while/body/eval_jaxpr/vmap(rhd,shd->hrs)/dot_general | solution.py:46
  199.0 14.1 %fusion.92 = (f32[8,8,64]{2,1,0:T(8,128)S(1)}, f32[8,8,64,576]{3,2,1,0:T(8,128)}) fusion(f32[8,8,64,576]{3,2,1,0:T(8,128)} %fusion.91, pred[8,576]{1,0:T(8,128)(4,1)S(1)} %broadcast_in_dim.75), kind=kOutput, calls=%fused_computation.105.clone.1.clone | output fusion | flops 14156351 | bytes 18895360 | tf_op jit(solution)/shard_map/while/body/eval_jaxpr/vmap()/sub | solution.py:51
  213.1 7.7 %copy.84 = bf16[8,576,512]{1,2,0:T(8,128)(2,1)} copy(bf16[8,576,512]{2,1,0:T(8,128)(2,1)} %get-tuple-element.231) | data formatting | bytes 9437184 | tf_op jit(solution)/shard_map/while/body/eval_jaxpr/vmap()/slice | solution.py:78
  220.8 7.4 %fusion.93 = bf16[8,8,64,64]{3,2,1,0:T(8,128)(2,1)S(1)} fusion(bf16[8,576,8,64]{1,3,2,0:T(8,128)(2,1)} %bitcast.157, f32[8,8,64,576]{3,2,1,0:T(8,128)} %get-tuple-element.236, f32[8,8,64]{2,1,0:T(8,128)S(1)} %get-tuple-element.237), kind=kOutput, calls=%fused_computation.13.clone.1.clone | convolution fusion | flops 306970624 | bytes 14696448 | tf_op jit(solution)/shard_map/while/body/eval_jaxpr/vmap(hrs,shd->rhd)/dot_general | solution.py:53
  232.2 5.9 %constant_dynamic-slice_fusion.11 = (bf16[3,8,64,1024]{3,2,1,0:T(8,128)(2,1)S(1)}, bf16[3,8,64,1024]{3,2,1,0:T(8,128)(2,1)S(1)}, bf16[3,8,64,1024]{3,2,1,0:T(8,128)(2,1)S(1)}) fusion(bf16[6,10,64,1024]{3,2,1,0:T(8,128)(2,1)} %get-tuple-element.268, s32[]{:T(128)S(6)} %select_n.42, s32[]{:T(128)S(6)} %add.1074, s32[]{:T(128)S(6)} %add.1075), kind=kLoop, calls=%fused_computation.24.clone.1.clone | loop fusion | bytes 18874380 | tf_op jit(solution)/shard_map/while/body/eval_jaxpr/slice | solution.py:86
  238.1 3.9 copy_bitcast_fusion.7
  244.2 8.4 %pad_maximum_fusion.13 = bf16[3,3,8,64,1024]{4,3,1,0,2:T(8,128)(2,1)} fusion(bf16[3,1,8,64,1024]{4,3,1,0,2:T(8,128)(2,1)} %get-tuple-element.228, bf16[3,1,8,64,1024]{4,3,1,0,2:T(8,128)(2,1)} %get-tuple-element.229, bf16[3,1,8,64,1024]{4,3,1,0,2:T(8,128)(2,1)} %bitcast.156), kind=kLoop, calls=%fused_computation.4.clone.1.clone | loop fusion | flops 9437184 | bytes 18874368 | tf_op jit(solution)/shard_map/while/body/eval_jaxpr/stack | solution.py:86
  252.6 8.3 %fusion.90 = (bf16[8,576,512]{2,1,0:T(8,128)(2,1)}, bf16[8,576,512]{2,1,0:T(8,128)(2,1)}) fusion(bf16[8,576,1024]{2,1,0:T(8,128)(2,1)} %bitcast.153), kind=kLoop, calls=%fused_computation.104.clone.1.clone | loop fusion | bytes 18874368 | tf_op jit(solution)/shard_map/while/body/eval_jaxpr/vmap()/slice | solution.py:78
  260.9 7.7 %copy.85 = bf16[8,576,512]{1,2,0:T(8,128)(2,1)} copy(bf16[8,576,512]{2,1,0:T(8,128)(2,1)} %get-tuple-element.232) | data formatting | bytes 9437184 | tf_op jit(solution)/shard_map/while/body/eval_jaxpr/vmap()/slice | solution.py:78
  271.5 7.9 %fusion.91 = f32[8,8,64,576]{3,2,1,0:T(8,128)} fusion(bf16[8,576,8,64]{1,3,2,0:T(8,128)(2,1)} %bitcast.154, bf16[8,64,8,64]{3,2,1,0:T(8,128)(2,1)S(1)} %squeeze.9), kind=kOutput, calls=%fused_computation.16.clone.1.clone | convolution fusion | flops 301989888 | bytes 14680064 | tf_op jit(solution)/shard_map/while/body/eval_jaxpr/vmap(rhd,shd->hrs)/dot_general | solution.py:46
  280.5 14.1 %fusion.92 = (f32[8,8,64]{2,1,0:T(8,128)S(1)}, f32[8,8,64,576]{3,2,1,0:T(8,128)}) fusion(f32[8,8,64,576]{3,2,1,0:T(8,128)} %fusion.91, pred[8,576]{1,0:T(8,128)(4,1)S(1)} %broadcast_in_dim.75), kind=kOutput, calls=%fused_computation.105.clone.1.clone | output fusion | flops 14156351 | bytes 18895360 | tf_op jit(solution)/shard_map/while/body/eval_jaxpr/vmap()/sub | solution.py:51
  294.6 7.7 %copy.84 = bf16[8,576,512]{1,2,0:T(8,128)(2,1)} copy(bf16[8,576,512]{2,1,0:T(8,128)(2,1)} %get-tuple-element.231) | data formatting | bytes 9437184 | tf_op jit(solution)/shard_map/while/body/eval_jaxpr/vmap()/slice | solution.py:78
  302.3 7.4 %fusion.93 = bf16[8,8,64,64]{3,2,1,0:T(8,128)(2,1)S(1)} fusion(bf16[8,576,8,64]{1,3,2,0:T(8,128)(2,1)} %bitcast.157, f32[8,8,64,576]{3,2,1,0:T(8,128)} %get-tuple-element.236, f32[8,8,64]{2,1,0:T(8,128)S(1)} %get-tuple-element.237), kind=kOutput, calls=%fused_computation.13.clone.1.clone | convolution fusion | flops 306970624 | bytes 14696448 | tf_op jit(solution)/shard_map/while/body/eval_jaxpr/vmap(hrs,shd->rhd)/dot_general | solution.py:53
  313.7 5.8 %constant_dynamic-slice_fusion.11 = (bf16[3,8,64,1024]{3,2,1,0:T(8,128)(2,1)S(1)}, bf16[3,8,64,1024]{3,2,1,0:T(8,128)(2,1)S(1)}, bf16[3,8,64,1024]{3,2,1,0:T(8,128)(2,1)S(1)}) fusion(bf16[6,10,64,1024]{3,2,1,0:T(8,128)(2,1)} %get-tuple-element.268, s32[]{:T(128)S(6)} %select_n.42, s32[]{:T(128)S(6)} %add.1074, s32[]{:T(128)S(6)} %add.1075), kind=kLoop, calls=%fused_computation.24.clone.1.clone | loop fusion | bytes 18874380 | tf_op jit(solution)/shard_map/while/body/eval_jaxpr/slice | solution.py:86
  319.5 3.9 copy_bitcast_fusion.7
  325.5 8.4 %pad_maximum_fusion.13 = bf16[3,3,8,64,1024]{4,3,1,0,2:T(8,128)(2,1)} fusion(bf16[3,1,8,64,1024]{4,3,1,0,2:T(8,128)(2,1)} %get-tuple-element.228, bf16[3,1,8,64,1024]{4,3,1,0,2:T(8,128)(2,1)} %get-tuple-element.229, bf16[3,1,8,64,1024]{4,3,1,0,2:T(8,128)(2,1)} %bitcast.156), kind=kLoop, calls=%fused_computation.4.clone.1.clone | loop fusion | flops 9437184 | bytes 18874368 | tf_op jit(solution)/shard_map/while/body/eval_jaxpr/stack | solution.py:86
  333.9 8.3 %fusion.90 = (bf16[8,576,512]{2,1,0:T(8,128)(2,1)}, bf16[8,576,512]{2,1,0:T(8,128)(2,1)}) fusion(bf16[8,576,1024]{2,1,0:T(8,128)(2,1)} %bitcast.153), kind=kLoop, calls=%fused_computation.104.clone.1.clone | loop fusion | bytes 18874368 | tf_op jit(solution)/shard_map/while/body/eval_jaxpr/vmap()/slice | solution.py:78
  342.2 7.7 %copy.85 = bf16[8,576,512]{1,2,0:T(8,128)(2,1)} copy(bf16[8,576,512]{2,1,0:T(8,128)(2,1)} %get-tuple-element.232) | data formatting | bytes 9437184 | tf_op jit(solution)/shard_map/while/body/eval_jaxpr/vmap()/slice | solution.py:78
  352.8 7.9 %fusion.91 = f32[8,8,64,576]{3,2,1,0:T(8,128)} fusion(bf16[8,576,8,64]{1,3,2,0:T(8,128)(2,1)} %bitcast.154, bf16[8,64,8,64]{3,2,1,0:T(8,128)(2,1)S(1)} %squeeze.9), kind=kOutput, calls=%fused_computation.16.clone.1.clone | convolution fusion | flops 301989888 | bytes 14680064 | tf_op jit(solution)/shard_map/while/body/eval_jaxpr/vmap(rhd,shd->hrs)/dot_general | solution.py:46
  361.9 14.1 %fusion.92 = (f32[8,8,64]{2,1,0:T(8,128)S(1)}, f32[8,8,64,576]{3,2,1,0:T(8,128)}) fusion(f32[8,8,64,576]{3,2,1,0:T(8,128)} %fusion.91, pred[8,576]{1,0:T(8,128)(4,1)S(1)} %broadcast_in_dim.75), kind=kOutput, calls=%fused_computation.105.clone.1.clone | output fusion | flops 14156351 | bytes 18895360 | tf_op jit(solution)/shard_map/while/body/eval_jaxpr/vmap()/sub | solution.py:51
  375.9 7.7 %copy.84 = bf16[8,576,512]{1,2,0:T(8,128)(2,1)} copy(bf16[8,576,512]{2,1,0:T(8,128)(2,1)} %get-tuple-element.231) | data formatting | bytes 9437184 | tf_op jit(solution)/shard_map/while/body/eval_jaxpr/vmap()/slice | solution.py:78
  383.6 7.4 %fusion.93 = bf16[8,8,64,64]{3,2,1,0:T(8,128)(2,1)S(1)} fusion(bf16[8,576,8,64]{1,3,2,0:T(8,128)(2,1)} %bitcast.157, f32[8,8,64,576]{3,2,1,0:T(8,128)} %get-tuple-element.236, f32[8,8,64]{2,1,0:T(8,128)S(1)} %get-tuple-element.237), kind=kOutput, calls=%fused_computation.13.clone.1.clone | convolution fusion | flops 306970624 | bytes 14696448 | tf_op jit(solution)/shard_map/while/body/eval_jaxpr/vmap(hrs,shd->rhd)/dot_general | solution.py:53
  403.6 3.8 collective-permute-done.5
  407.6 3.7 collective-permute-start.6
  413.5 4.4 collective-permute-done.7
  417.9 3.7 maximum_maximum_fusion
  421.8 35.4 %fusion.51 = (f32[32,64]{1,0:T(8,128)S(1)}, f32[32,64,512]{2,1,0:T(8,128)S(1)}) fusion(f32[512]{0:T(512)S(1)} %copy-done.30, f32[512]{0:T(512)S(1)} %bitcast.215, bf16[38,67,512]{2,1,0:T(8,128)(2,1)S(1)} %get-tuple-element.97, f32[512]{0:T(512)S(1)} %bitcast.216, f32[512]{0:T(512)S(1)} %bitcast.169, f32[512]{0:T(512)S(1)} %bitcast.170, ...), kind=kLoop, calls=%fused_computation.103 | loop fusion | flops 161478656 | bytes 94875648 | tf_op jit(solution)/shard_map/reduce_sum | solution.py:26
  (160 shorter events, 69.3 us)
Async XLA Ops:
  0.0 5.6 %copy-start = (bf16[512,1536]{1,0:T(8,128)(2,1)S(1)}, bf16[512,1536]{1,0:T(8,128)(2,1)}, u32[]{:S(2)}) copy-start(bf16[512,1536]{1,0:T(8,128)(2,1)} %param.13) | copy-start | bytes 4718596
  0.0 4.6 %copy-start.3 = (bf16[32,64,512]{2,1,0:T(8,128)(2,1)S(1)}, bf16[32,64,512]{2,1,0:T(8,128)(2,1)}, u32[]{:S(2)}) copy-start(bf16[32,64,512]{2,1,0:T(8,128)(2,1)} %param.10) | copy-start | bytes 6291460
  0.0 4.7 %copy-start.29 = (f32[512]{0:T(512)S(1)}, f32[512]{0:T(512)}, u32[]{:S(2)}) copy-start(f32[512]{0:T(512)} %param.12) | copy-start | bytes 6148
  9.5 25.8 %collective-permute-start = (bf16[8,64,1024]{2,1,0:T(8,128)(2,1)S(1)}, bf16[8,64,1024]{2,1,0:T(8,128)(2,1)S(1)}, u32[]{:S(2)}, u32[]{:S(2)}) collective-permute-start(bf16[8,64,1024]{2,1,0:T(8,128)(2,1)S(1)} %get-tuple-element.94), channel_id=1, source_target_pairs={{0,4},{4,8},{8,12},{1,5},{5,9},{9,13},{2,6},{6,10},{10,14},{3,7},{... | collective-permute-start | bytes 3145736 | tf_op jit(solution)/shard_map/ppermute | solution.py:19
  13.6 25.6 %collective-permute-start.1 = (bf16[8,64,1024]{2,1,0:T(8,128)(2,1)S(1)}, bf16[8,64,1024]{2,1,0:T(8,128)(2,1)S(1)}, u32[]{:S(2)}, u32[]{:S(2)}) collective-permute-start(bf16[8,64,1024]{2,1,0:T(8,128)(2,1)S(1)} %get-tuple-element.95), channel_id=1, source_target_pairs={{4,0},{8,4},{12,8},{5,1},{9,5},{13,9},{6,2},{10,6},{14,10},{7,3},{... | collective-permute-start | bytes 3145736 | tf_op jit(solution)/shard_map/ppermute | solution.py:20
  15.4 23.8 %copy-start.2 = (bf16[32,64,1024]{2,1,0:T(8,128)(2,1)}, bf16[32,64,1024]{2,1,0:T(8,128)(2,1)S(1)}, u32[]{:S(2)}) copy-start(bf16[32,64,1024]{2,1,0:T(8,128)(2,1)S(1)} %slice.509) | copy-start | bytes 12582916
  15.4 33.3 %copy-start.28 = (s32[4,4,24]{2,1,0:T(4,128)S(1)}, s32[4,4,24]{2,1,0:T(4,128)}, u32[]{:S(2)}) copy-start(s32[4,4,24]{2,1,0:T(4,128)} %param.11) | copy-start | bytes 4612
  39.2 1.2 copy-start.6
  40.4 15.6 %collective-permute-start.2 = (bf16[48,8,1024]{2,1,0:T(8,128)(2,1)}, bf16[48,8,1024]{2,1,0:T(8,128)(2,1)S(1)}, u32[]{:S(2)}, u32[]{:S(2)}) collective-permute-start(bf16[48,8,1024]{2,1,0:T(8,128)(2,1)} %get-tuple-element.92), channel_id=1, source_target_pairs={{0,1},{1,2},{2,3},{4,5},{5,6},{6,7},{8,9},{9,10},{10,11},{12,13},{... | collective-permute-start | bytes 2359304 | tf_op jit(solution)/shard_map/ppermute | solution.py:19
  45.3 13.4 %collective-permute-start.3 = (bf16[48,8,1024]{2,1,0:T(8,128)(2,1)S(1)}, bf16[48,8,1024]{2,1,0:T(8,128)(2,1)}, u32[]{:S(2)}, u32[]{:S(2)}) collective-permute-start(bf16[48,8,1024]{2,1,0:T(8,128)(2,1)S(1)} %get-tuple-element.93), channel_id=1, source_target_pairs={{1,0},{2,1},{3,2},{5,4},{6,5},{7,6},{9,8},{10,9},{11,10},{13,12},{... | collective-permute-start | bytes 2359304 | tf_op jit(solution)/shard_map/ppermute | solution.py:20
  56.0 0.9 copy-start.7
  66.9 325.6 %copy-start.32 = (pred[4,8]{1,0:T(4,128)(4,1)S(1)}, pred[4,8]{1,0:T(4,128)(4,1)}, u32[]{:S(2)}) copy-start(pred[4,8]{1,0:T(4,128)(4,1)} %slice.398) | copy-start | bytes 100
  139.4 7.5 %copy-start.5 = (bf16[512,512]{1,0:T(8,128)(2,1)S(1)}, bf16[512,512]{1,0:T(8,128)(2,1)}, u32[]{:S(2)}) copy-start(bf16[512,512]{1,0:T(8,128)(2,1)} %get-tuple-element.271) | copy-start | bytes 1572868 | tf_op jit(solution)/shard_map/while
  220.8 7.5 %copy-start.5 = (bf16[512,512]{1,0:T(8,128)(2,1)S(1)}, bf16[512,512]{1,0:T(8,128)(2,1)}, u32[]{:S(2)}) copy-start(bf16[512,512]{1,0:T(8,128)(2,1)} %get-tuple-element.271) | copy-start | bytes 1572868 | tf_op jit(solution)/shard_map/while
  302.3 7.5 %copy-start.5 = (bf16[512,512]{1,0:T(8,128)(2,1)S(1)}, bf16[512,512]{1,0:T(8,128)(2,1)}, u32[]{:S(2)}) copy-start(bf16[512,512]{1,0:T(8,128)(2,1)} %get-tuple-element.271) | copy-start | bytes 1572868 | tf_op jit(solution)/shard_map/while
  383.6 7.5 %copy-start.5 = (bf16[512,512]{1,0:T(8,128)(2,1)S(1)}, bf16[512,512]{1,0:T(8,128)(2,1)}, u32[]{:S(2)}) copy-start(bf16[512,512]{1,0:T(8,128)(2,1)} %get-tuple-element.271) | copy-start | bytes 1572868 | tf_op jit(solution)/shard_map/while
  395.4 1.6 copy-start.4
  397.0 5.3 %copy-start.8 = (f32[7,7,512]{2,1,0:T(8,128)S(1)}, f32[7,7,512]{2,1,0:T(8,128)}, u32[]{:S(2)}) copy-start(f32[7,7,512]{2,1,0:T(8,128)} %param.15) | copy-start | bytes 301060
  397.9 5.7 %collective-permute-start.4 = (bf16[3,64,512]{2,1,0:T(8,128)(2,1)S(1)}, bf16[3,64,512]{2,1,0:T(8,128)(2,1)S(1)}, u32[]{:S(2)}, u32[]{:S(2)}) collective-permute-start(bf16[3,64,512]{2,1,0:T(8,128)(2,1)S(1)} %get-tuple-element.100), channel_id=1, source_target_pairs={{0,4},{4,8},{8,12},{1,5},{5,9},{9,13},{2,6},{6,10},{10,14},{3,7},{... | collective-permute-start | bytes 589832 | tf_op jit(solution)/shard_map/ppermute | solution.py:19
  401.1 6.4 %collective-permute-start.5 = (bf16[3,64,512]{2,1,0:T(8,128)(2,1)S(1)}, bf16[3,64,512]{2,1,0:T(8,128)(2,1)S(1)}, u32[]{:S(2)}, u32[]{:S(2)}) collective-permute-start(bf16[3,64,512]{2,1,0:T(8,128)(2,1)S(1)} %get-tuple-element.101), channel_id=1, source_target_pairs={{4,0},{8,4},{12,8},{5,1},{9,5},{13,9},{6,2},{10,6},{14,10},{7,3},{... | collective-permute-start | bytes 589832 | tf_op jit(solution)/shard_map/ppermute | solution.py:20
  407.6 5.9 %collective-permute-start.6 = (bf16[38,3,512]{2,1,0:T(4,128)(2,1)S(1)}, bf16[38,3,512]{2,1,0:T(4,128)(2,1)S(1)}, u32[]{:S(2)}, u32[]{:S(2)}) collective-permute-start(bf16[38,3,512]{2,1,0:T(4,128)(2,1)S(1)} %get-tuple-element.98), channel_id=1, source_target_pairs={{0,1},{1,2},{2,3},{4,5},{5,6},{6,7},{8,9},{9,10},{10,11},{12,13},{... | collective-permute-start | bytes 350216 | tf_op jit(solution)/shard_map/ppermute | solution.py:19
  411.4 6.5 %collective-permute-start.7 = (bf16[38,3,512]{2,1,0:T(4,128)(2,1)S(1)}, bf16[38,3,512]{2,1,0:T(4,128)(2,1)S(1)}, u32[]{:S(2)}, u32[]{:S(2)}) collective-permute-start(bf16[38,3,512]{2,1,0:T(4,128)(2,1)S(1)} %get-tuple-element.99), channel_id=1, source_target_pairs={{1,0},{2,1},{3,2},{5,4},{6,5},{7,6},{9,8},{10,9},{11,10},{13,12},{... | collective-permute-start | bytes 350216 | tf_op jit(solution)/shard_map/ppermute | solution.py:20
  413.3 8.3 %copy-start.9 = (f32[1,1,512]{2,1,0:T(1,128)S(1)}, f32[1,1,512]{2,1,0:T(1,128)}, u32[]{:S(2)}) copy-start(f32[1,1,512]{2,1,0:T(1,128)} %get-tuple-element.102) | copy-start | bytes 6148
  413.3 8.3 %copy-start.10 = (f32[1,1,512]{2,1,0:T(1,128)S(1)}, f32[1,1,512]{2,1,0:T(1,128)}, u32[]{:S(2)}) copy-start(f32[1,1,512]{2,1,0:T(1,128)} %get-tuple-element.103) | copy-start | bytes 6148
  413.3 8.3 %copy-start.11 = (f32[1,1,512]{2,1,0:T(1,128)S(1)}, f32[1,1,512]{2,1,0:T(1,128)}, u32[]{:S(2)}) copy-start(f32[1,1,512]{2,1,0:T(1,128)} %get-tuple-element.104) | copy-start | bytes 6148
  413.3 8.3 %copy-start.12 = (f32[1,1,512]{2,1,0:T(1,128)S(1)}, f32[1,1,512]{2,1,0:T(1,128)}, u32[]{:S(2)}) copy-start(f32[1,1,512]{2,1,0:T(1,128)} %get-tuple-element.105) | copy-start | bytes 6148
  413.3 8.3 %copy-start.13 = (f32[1,1,512]{2,1,0:T(1,128)S(1)}, f32[1,1,512]{2,1,0:T(1,128)}, u32[]{:S(2)}) copy-start(f32[1,1,512]{2,1,0:T(1,128)} %get-tuple-element.106) | copy-start | bytes 6148
  413.4 8.3 %copy-start.14 = (f32[1,1,512]{2,1,0:T(1,128)S(1)}, f32[1,1,512]{2,1,0:T(1,128)}, u32[]{:S(2)}) copy-start(f32[1,1,512]{2,1,0:T(1,128)} %get-tuple-element.107) | copy-start | bytes 6148
  413.4 8.3 %copy-start.15 = (f32[1,1,512]{2,1,0:T(1,128)S(1)}, f32[1,1,512]{2,1,0:T(1,128)}, u32[]{:S(2)}) copy-start(f32[1,1,512]{2,1,0:T(1,128)} %get-tuple-element.108) | copy-start | bytes 6148
  413.4 8.3 %copy-start.16 = (f32[1,1,512]{2,1,0:T(1,128)S(1)}, f32[1,1,512]{2,1,0:T(1,128)}, u32[]{:S(2)}) copy-start(f32[1,1,512]{2,1,0:T(1,128)} %get-tuple-element.109) | copy-start | bytes 6148
  413.4 8.3 %copy-start.17 = (f32[1,1,512]{2,1,0:T(1,128)S(1)}, f32[1,1,512]{2,1,0:T(1,128)}, u32[]{:S(2)}) copy-start(f32[1,1,512]{2,1,0:T(1,128)} %get-tuple-element.110) | copy-start | bytes 6148
  413.4 8.3 %copy-start.18 = (f32[1,1,512]{2,1,0:T(1,128)S(1)}, f32[1,1,512]{2,1,0:T(1,128)}, u32[]{:S(2)}) copy-start(f32[1,1,512]{2,1,0:T(1,128)} %get-tuple-element.111) | copy-start | bytes 6148
  413.4 8.3 %copy-start.19 = (f32[1,1,512]{2,1,0:T(1,128)S(1)}, f32[1,1,512]{2,1,0:T(1,128)}, u32[]{:S(2)}) copy-start(f32[1,1,512]{2,1,0:T(1,128)} %get-tuple-element.112) | copy-start | bytes 6148
  413.4 8.3 %copy-start.20 = (f32[1,1,512]{2,1,0:T(1,128)S(1)}, f32[1,1,512]{2,1,0:T(1,128)}, u32[]{:S(2)}) copy-start(f32[1,1,512]{2,1,0:T(1,128)} %get-tuple-element.113) | copy-start | bytes 6148
  413.4 8.3 %copy-start.21 = (f32[1,1,512]{2,1,0:T(1,128)S(1)}, f32[1,1,512]{2,1,0:T(1,128)}, u32[]{:S(2)}) copy-start(f32[1,1,512]{2,1,0:T(1,128)} %get-tuple-element.114) | copy-start | bytes 6148
  413.4 8.3 %copy-start.22 = (f32[1,1,512]{2,1,0:T(1,128)S(1)}, f32[1,1,512]{2,1,0:T(1,128)}, u32[]{:S(2)}) copy-start(f32[1,1,512]{2,1,0:T(1,128)} %get-tuple-element.115) | copy-start | bytes 6148
  413.4 8.3 %copy-start.23 = (f32[1,1,512]{2,1,0:T(1,128)S(1)}, f32[1,1,512]{2,1,0:T(1,128)}, u32[]{:S(2)}) copy-start(f32[1,1,512]{2,1,0:T(1,128)} %get-tuple-element.116) | copy-start | bytes 6148
  413.5 8.3 %copy-start.24 = (f32[1,1,512]{2,1,0:T(1,128)S(1)}, f32[1,1,512]{2,1,0:T(1,128)}, u32[]{:S(2)}) copy-start(f32[1,1,512]{2,1,0:T(1,128)} %get-tuple-element.117) | copy-start | bytes 6148
  413.5 8.3 %copy-start.25 = (f32[1,1,512]{2,1,0:T(1,128)S(1)}, f32[1,1,512]{2,1,0:T(1,128)}, u32[]{:S(2)}) copy-start(f32[1,1,512]{2,1,0:T(1,128)} %get-tuple-element.118) | copy-start | bytes 6148
  413.5 8.3 %copy-start.26 = (f32[1,1,512]{2,1,0:T(1,128)S(1)}, f32[1,1,512]{2,1,0:T(1,128)}, u32[]{:S(2)}) copy-start(f32[1,1,512]{2,1,0:T(1,128)} %get-tuple-element.119) | copy-start | bytes 6148
  413.5 8.3 %copy-start.27 = (f32[1,1,512]{2,1,0:T(1,128)S(1)}, f32[1,1,512]{2,1,0:T(1,128)}, u32[]{:S(2)}) copy-start(f32[1,1,512]{2,1,0:T(1,128)} %get-tuple-element.120) | copy-start | bytes 6148
  413.5 8.3 %copy-start.30 = (f32[512]{0:T(512)S(1)}, f32[512]{0:T(512)}, u32[]{:S(2)}) copy-start(f32[512]{0:T(512)} %param.16) | copy-start | bytes 6148
  457.2 0.9 copy-start.31
  458.0 2.0 copy-start.1
where the time goes:
time: 462 us; the launch traced here: 460 us
  local copies, waits for them, and re-layouts  172 us (37%)
  other arithmetic  147 us (32%)
  matrix products  70.6 us (15%)
  waiting for transfers between devices  35 us (8%)
  starting transfers between devices  22.3 us (5%)
  loops' own time  13.2 us (3%)
    slice x12, local copies, waits for them, and re-layouts, finish(): out = attend(query_block, window[:, :width], window[:, width:], key_ok)  94.6 us
    sub x4, other arithmetic, attend(): weights = jnp.exp(scores - top)  56.3 us
    reduce_sum x2, other arithmetic, layer_norm(): mean = jnp.mean(values, axis=-1, keepdims=True)  37.5 us
    another operation x4, other arithmetic, block_row(): window = jnp.stack([near[:, b:b + BC] for b in range(3)], axis=1)  33.7 us
    dot_general x4, matrix products, attend(): jnp.einsum('rhd,shd->hrs', qh, kh, preferred_element_type=jnp.float32)  31.5 us
    dot_general x4, matrix products, attend(): jnp.einsum('hrs,shd->rhd', probs, vh, preferred_element_type=jnp.float32)  29.8 us
    slice x4, local copies, waits for them, and re-layouts, block_row(): window = jnp.stack([near[:, b:b + BC] for b in range(3)], axis=1)  23.4 us
    ppermute x4, waiting for transfers between devices, with_halo(): before = lax.ppermute(last, axis, up)  21.1 us
  transfers between devices with their start and end apart: 8, of which 6 were waited for; matrix products, arithmetic and copies ran while one was open for 2% of the time, Pallas kernels for 0%

commit v1 on v0

v1 whole, which is shorter than its diff:
```python
import functools

import jax
import jax.numpy as jnp
from jax import lax
from jax.experimental import pallas as pl
from jax.experimental.pallas import tpu as pltpu
from jax.sharding import PartitionSpec as P

HEADS = 8
BLK = 8
BR = 4
BC = 8
GROUP = 4
SIDES = ((-1, 0), (1, 0), (0, -1), (0, 1), (-1, -1), (-1, 1), (1, -1), (1, 1))
VM = pl.BlockSpec(memory_space=pltpu.VMEM)
SM = pl.BlockSpec(memory_space=pltpu.SMEM)
ANY = pl.BlockSpec(memory_space=pl.ANY)
MIB = 1024 * 1024


def block_table(tissue_list):
    tiles_r, tiles_c, slots = tissue_list.shape
    hits = jnp.any(tissue_list[..., None] == jnp.arange(BR * BC, dtype=jnp.int32), axis=2)
    hits = hits.reshape(tiles_r, tiles_c, BR, BC).transpose(0, 2, 1, 3)
    return hits.reshape(tiles_r * BR, tiles_c * BC)


def exchange(sizes, views, send_sems, recv_sems):
    n_r, n_c = sizes
    r, c = lax.axis_index("row"), lax.axis_index("col")
    barrier = pltpu.get_barrier_semaphore()

    def there(dr, dc):
        ok = None
        for at, step, n in ((r, dr, n_r), (c, dc, n_c)):
            if step == -1:
                one = at > 0
            elif step == 1:
                one = at < n - 1
            else:
                continue
            ok = one if ok is None else jnp.logical_and(ok, one)
        return ok

    def target(dr, dc):
        return {"row": r + dr, "col": c + dc}

    for dr, dc in SIDES:
        @pl.when(there(dr, dc))
        def _():
            pl.semaphore_signal(
                barrier, inc=1, device_id=target(dr, dc), device_id_type=pl.DeviceIdType.MESH
            )

    peers = sum(there(dr, dc).astype(jnp.int32) for dr, dc in SIDES)
    pl.semaphore_wait(barrier, peers)

    def copy(k):
        dr, dc = SIDES[k]
        src, dst = views(dr, dc)
        return pltpu.make_async_remote_copy(
            src_ref=src,
            dst_ref=dst,
            send_sem=send_sems.at[k],
            recv_sem=recv_sems.at[k],
            device_id=target(dr, dc),
            device_id_type=pl.DeviceIdType.MESH,
        )

    for k, (dr, dc) in enumerate(SIDES):
        @pl.when(there(dr, dc))
        def _():
            copy(k).start()

    def finish():
        for k, (dr, dc) in enumerate(SIDES):
            @pl.when(there(dr, dc))
            def _():
                copy(k).wait_send()

            @pl.when(there(-dr, -dc))
            def _():
                copy(k).wait_recv()

    return finish


def token_halo_kernel(sizes, blocks, frame, send_sems, recv_sems, own_sem):
    def span(step, n):
        if step == -1:
            return pl.ds(0, 1), pl.ds(n + 1, 1)
        if step == 1:
            return pl.ds(n - 1, 1), pl.ds(0, 1)
        return pl.ds(0, n), pl.ds(1, n)

    def views(dr, dc):
        (sr, tr), (sc, tc) = span(dr, BR), span(dc, BC)
        return blocks.at[sr, sc], frame.at[tr, tc]

    own = pltpu.make_async_copy(blocks, frame.at[pl.ds(1, BR), pl.ds(1, BC)], own_sem)
    own.start()
    finish = exchange(sizes, views, send_sems, recv_sems)
    own.wait()
    finish()


def mixed_halo_kernel(
    sizes, mixed, edges, top, bottom, sides, corners, send_sems, recv_sems
):
    height = mixed.shape[0]
    tall = edges.shape[1]

    def views(dr, dc):
        if dc == 0:
            if dr == -1:
                return mixed.at[pl.ds(0, 3)], bottom
            return mixed.at[pl.ds(height - 3, 3)], top
        mine = 0 if dc == -1 else 1
        if dr == 0:
            return edges.at[mine], sides.at[1 - mine]
        rows = pl.ds(0, 32) if dr == -1 else pl.ds(tall - 32, 32)
        place = (2 if dr == -1 else 0) + 1 - mine
        return edges.at[mine, rows], corners.at[place]

    exchange(sizes, views, send_sems, recv_sems)()


def attention_kernel(
    ok_ref, frame, gain, w_qkv, w_out, bias, mixed, edges, qkv, normed, att, mix
):
    width = frame.shape[-1]
    tok = BLK * BLK
    half = width // 2
    head = width // HEADS

    def project(i, carry):
        for j in range(BC + 2):
            x = frame[i, j].astype(jnp.float32)
            x = jnp.where(ok_ref[i, j] != 0, x, 0.0)
            cent = x - jnp.mean(x, axis=-1, keepdims=True)
            var = jnp.mean(cent * cent, axis=-1, keepdims=True)
            y = cent * lax.rsqrt(var + 1e-06) * gain[...]
            normed[pl.ds(j * tok, tok), :] = y.astype(jnp.bfloat16)
        for n in range(3):
            cols = pl.ds(n * width, width)
            p = jnp.dot(normed[...], w_qkv[:, cols], preferred_element_type=jnp.float32)
            qkv[i, :, :, cols] = p.astype(jnp.bfloat16).reshape(BC + 2, tok, width)
        return carry

    lax.fori_loop(0, BR + 2, project, 0)

    shape = (GROUP * tok, half)
    same = (
        lax.broadcasted_iota(jnp.int32, shape, 0) // tok
        == lax.broadcasted_iota(jnp.int32, shape, 1) // head
    )

    def attend(b, carry):
        bi = b // BC
        bj = b % BC
        ok = ok_ref[bi + 1, bj + 1] != 0

        @pl.when(ok)
        def _():
            for g in range(2):
                q = qkv[bi + 1, bj + 1, :, pl.ds(g * half, half)].astype(jnp.float32)
                q = q * head ** (-0.5)
                q = jnp.where(same, jnp.concatenate([q] * GROUP, axis=0), 0.0)
                q = q.astype(jnp.bfloat16)

                def window(start):
                    return jnp.concatenate(
                        [
                            qkv[bi + a, pl.ds(bj, 3), :, pl.ds(start, half)].reshape(
                                3 * tok, half
                            )
                            for a in range(3)
                        ],
                        axis=0,
                    )

                s = lax.dot_general(
                    q,
                    window(width + g * half),
                    (((1,), (1,)), ((), ())),
                    preferred_element_type=jnp.float32,
                )
                s = s + bias[b]
                e = jnp.exp(s - jnp.max(s, axis=-1, keepdims=True))
                total = jnp.sum(e, axis=-1, keepdims=True)
                o = jnp.dot(
                    e.astype(jnp.bfloat16),
                    window(2 * width + g * half),
                    preferred_element_type=jnp.float32,
                )
                o = jnp.where(same, o * (1.0 / total), 0.0)
                o = o[:tok] + o[tok : 2 * tok] + o[2 * tok : 3 * tok] + o[3 * tok :]
                att[b, :, pl.ds(g * half, half)] = o.astype(jnp.bfloat16)

        @pl.when(jnp.logical_not(ok))
        def _():
            att[b] = jnp.zeros((tok, width), jnp.bfloat16)

        return carry

    lax.fori_loop(0, BR * BC, attend, 0)

    def out(bi, carry):
        a = att[pl.ds(bi * BC, BC)].reshape(BC * tok, width)
        d = jnp.dot(a, w_out[...], preferred_element_type=jnp.float32)
        rows = pl.ds(bi * BLK, BLK)
        for bj in range(BC):
            m = frame[bi + 1, bj + 1].astype(jnp.float32) + d[bj * tok : (bj + 1) * tok]
            mix[rows, pl.ds(bj * BLK, BLK), :] = m.reshape(BLK, BLK, width)
        mixed[rows] = mix[rows].astype(jnp.bfloat16)
        for side, start in ((0, 0), (1, (BC - 1) * BLK)):
            m = mix[rows, pl.ds(start, BLK), :].reshape(tok, width)
            edges[side, pl.ds(bi * tok, tok), :] = m.astype(jnp.bfloat16)
        return carry

    lax.fori_loop(0, BR, out, 0)


def conv_kernel(
    flags, mixed, top, bottom, sides, corners, weight, bias, gain, out, framed, filt
):
    height, breadth, width = mixed.shape
    up, down, left, right = [flags[k] != 0 for k in range(4)]
    f32 = jnp.float32

    def fill(i, carry):
        rows = pl.ds(i * BLK, BLK)
        framed[pl.ds(i * BLK + 3, BLK), pl.ds(8, breadth), :] = mixed[rows].astype(f32)
        for k, ok, start in ((0, left, 0), (1, right, breadth + 8)):
            v = sides[k, pl.ds(i * BLK * 8, BLK * 8), :].astype(f32)
            framed[pl.ds(i * BLK + 3, BLK), pl.ds(start, 8), :] = jnp.where(ok, v, 0.0).reshape(
                BLK, 8, width
            )
        return carry

    lax.fori_loop(0, height // BLK, fill, 0)
    for k, ok, ref, start in ((0, up, top, 0), (2, down, bottom, height + 3)):
        rows = pl.ds(start, 3)
        framed[rows, pl.ds(8, breadth), :] = jnp.where(ok, ref[...].astype(f32), 0.0)
        for h, side_ok, col in ((0, left, 0), (1, right, breadth + 8)):
            v = corners[k + h].astype(f32).reshape(4, 8, width)
            v = v[1:] if k == 0 else v[:3]
            both = jnp.logical_and(ok, side_ok)
            framed[rows, pl.ds(col, 8), :] = jnp.where(both, v, 0.0)

    def row_block(i, carry):
        r0 = i * BLK

        def lanes(l, inner):
            lane = pl.ds(pl.multiple_of(l * 128, 128), 128)
            for c0 in range(0, breadth, 8):
                acc = jnp.zeros((BLK, 8, 128), f32) + bias[:, lane]
                for dx in range(7):
                    v = framed[pl.ds(r0, BLK + 6), pl.ds(c0 + dx + 5, 8), lane]
                    for dy in range(7):
                        acc = acc + v[dy : dy + BLK] * weight[dy * 7 + dx, :, lane]
                filt[:, pl.ds(c0, 8), lane] = acc
            return inner

        lax.fori_loop(0, width // 128, lanes, 0)

        def norm(y, inner):
            f = filt[y]
            cent = f - jnp.mean(f, axis=-1, keepdims=True)
            var = jnp.mean(cent * cent, axis=-1, keepdims=True)
            branch = cent * lax.rsqrt(var + 1e-06) * gain[...]
            out[r0 + y] = (mixed[r0 + y].astype(f32) + branch).astype(jnp.bfloat16)
            return inner

        lax.fori_loop(0, BLK, norm, 0)
        return carry

    lax.fori_loop(0, height // BLK, row_block, 0)


def per_device(tokens, tissue_list, ln_gain, w_qkv, w_out, conv_weight, conv_bias, conv_gain):
    height, breadth, width = tokens.shape
    tok = BLK * BLK
    bf16, f32 = jnp.bfloat16, jnp.float32
    sizes = (lax.axis_size("row"), lax.axis_size("col"))
    row, col = lax.axis_index("row"), lax.axis_index("col")
    dma = pltpu.SemaphoreType.DMA

    blocks = tokens.reshape(BR, BLK, BC, BLK, width).transpose(0, 2, 1, 3, 4)
    blocks = blocks.reshape(BR, BC, tok, width)
    frame = pl.pallas_call(
        functools.partial(token_halo_kernel, sizes),
        out_shape=jax.ShapeDtypeStruct((BR + 2, BC + 2, tok, width), bf16),
        in_specs=[ANY],
        out_specs=ANY,
        scratch_shapes=[dma((8,)), dma((8,)), dma],
        compiler_params=pltpu.CompilerParams(collective_id=0, has_side_effects=True),
    )(blocks)

    table = jnp.pad(block_table(tissue_list), 1)
    near = lax.dynamic_slice(table, (row * BR, col * BC), (BR + 2, BC + 2))
    okay = jnp.stack(
        [near[a : a + BR, b : b + BC] for a in range(3) for b in range(3)], axis=-1
    ).reshape(BR * BC, 1, 9)
    bias = jnp.repeat(jnp.where(okay, 0.0, -1e30).astype(f32), tok, axis=-1)

    mixed, edges = pl.pallas_call(
        attention_kernel,
        out_shape=(
            jax.ShapeDtypeStruct((height, breadth, width), bf16),
            jax.ShapeDtypeStruct((2, height * 8, width), bf16),
        ),
        in_specs=[SM, VM, VM, VM, VM, VM],
        out_specs=(VM, VM),
        scratch_shapes=[
            pltpu.VMEM((BR + 2, BC + 2, tok, 3 * width), bf16),
            pltpu.VMEM(((BC + 2) * tok, width), bf16),
            pltpu.VMEM((BR * BC, tok, width), bf16),
            pltpu.VMEM((height, breadth, width), f32),
        ],
        compiler_params=pltpu.CompilerParams(vmem_limit_bytes=50 * MIB),
    )(near.astype(jnp.int32), frame, ln_gain.reshape(1, width), w_qkv, w_out, bias)

    top, bottom, sides, corners = pl.pallas_call(
        functools.partial(mixed_halo_kernel, sizes),
        out_shape=(
            jax.ShapeDtypeStruct((3, breadth, width), bf16),
            jax.ShapeDtypeStruct((3, breadth, width), bf16),
            jax.ShapeDtypeStruct((2, height * 8, width), bf16),
            jax.ShapeDtypeStruct((4, 32, width), bf16),
        ),
        in_specs=[ANY, ANY],
        out_specs=(ANY,) * 4,
        scratch_shapes=[dma((8,)), dma((8,))],
        compiler_params=pltpu.CompilerParams(collective_id=1, has_side_effects=True),
    )(mixed, edges)

    flags = jnp.stack([row > 0, row < sizes[0] - 1, col > 0, col < sizes[1] - 1])
    weight = jnp.broadcast_to(conv_weight.reshape(49, 1, width), (49, 8, width))
    return pl.pallas_call(
        conv_kernel,
        out_shape=jax.ShapeDtypeStruct((height, breadth, width), bf16),
        in_specs=[SM] + [VM] * 8,
        out_specs=VM,
        scratch_shapes=[
            pltpu.VMEM((height + 6, breadth + 16, width), f32),
            pltpu.VMEM((BLK, breadth, width), f32),
        ],
        compiler_params=pltpu.CompilerParams(vmem_limit_bytes=40 * MIB),
    )(
        flags.astype(jnp.int32),
        mixed,
        top,
        bottom,
        sides,
        corners,
        weight,
        conv_bias.reshape(1, width),
        conv_gain.reshape(1, width),
    )


def solution(mesh):
    tile = P(("slide", "row"), "col", None)
    in_specs = (tile, P("slide", None, None), P(), P(), P(), P(), P(), P())
    return jax.shard_map(
        per_device, mesh=mesh, in_specs=in_specs, out_specs=tile, check_vma=False
    )
```

time: 462 us -> 180 us (0.39)
  Pallas kernels: 0 us -> 168 us
  local copies, waits for them, and re-layouts: 172 us -> 9.37 us
  other arithmetic: 147 us -> 1 us
  matrix products: 70.6 us -> 0 us
  waiting for transfers between devices: 35 us -> 0 us
  starting transfers between devices: 22.3 us -> 0 us
  loops' own time: 13.2 us -> 0 us
    pallas_call x0 -> x4, Pallas kernels: none -> 168 us  [the longest x1 64.8 us: per_device(): pl.pallas_call(functools.partial(token_halo_kernel, sizes), out_shape=jax...]
    slice x24 -> x1, local copies, waits for them, and re-layouts: 123 us -> 0.08 us  [per_device(): near[a:a + BR, b:b + BC]]
    dot_general x13 -> x0, matrix products: 70.6 us -> none  [the longest x4 31.5 us: attend(): jnp.einsum('rhd,shd->hrs', qh, kh, preferred_element_type=jnp.float32)]
    sub x4 -> x0, other arithmetic: 56.3 us -> none  [attend(): weights = jnp.exp(scores - top)]
    reduce_sum x4 -> x0, other arithmetic: 40.8 us -> none  [the longest x2 37.5 us: layer_norm(): mean = jnp.mean(values, axis=-1, keepdims=True)]
    ppermute x8 -> x0, waiting for transfers between devices: 35 us -> none  [the longest x4 21.1 us: with_halo(): before = lax.ppermute(last, axis, up)]
    another operation x4 -> x0, other arithmetic: 33.7 us -> none  [block_row(): window = jnp.stack([near[:, b:b + BC] for b in range(3)], axis=1)]
    ppermute x8 -> x0, starting transfers between devices: 22.3 us -> none  [the longest x4 15.8 us: with_halo(): before = lax.ppermute(last, axis, up)]
  transfers between devices with their start and end apart: 8 -> 0, of which waited for: 6 -> 0; matrix products, arithmetic and copies ran while one was open for 2% -> 0% of each run, Pallas kernels for 0% -> 0%
where the time goes in v1:
time: 180 us; the launch traced here: 179 us
  Pallas kernels  168 us (93%)
  local copies, waits for them, and re-layouts  9.37 us (5%)
    pallas_call x1, Pallas kernels, per_device(): pl.pallas_call(functools.partial(token_halo_kernel, sizes), out_shape=jax...  64.8 us
    pallas_call x1, Pallas kernels, per_device(): pl.pallas_call(conv_kernel, out_shape=jax.ShapeDtypeStruct((height, bread...  56.3 us
    pallas_call x1, Pallas kernels, per_device(): pl.pallas_call(attention_kernel, out_shape=(jax.ShapeDtypeStruct((height,...  32.2 us
    pallas_call x1, Pallas kernels, per_device(): pl.pallas_call(functools.partial(mixed_halo_kernel, sizes), out_shape=(ja...  14.7 us
    unnamed x24, local copies, waits for them, and re-layouts  4.61 us

profile of v1, /device:TPU:1, one launch (start us, length us, event | category | flops | bytes accessed | tf_op | source)
XLA Modules:
  0.0 178.5 jit_solution(330942871658368210)
XLA Ops:
  0.0 0.1 add_convert_fusion.flags
  0.1 0.8 fusion
  0.9 0.1 reshape.86
  1.0 0.1 reshape.87
  1.1 0.1 fusion.1
  1.2 3.2 %copy.20 = bf16[4,8,8,8,512]{4,3,1,2,0:T(8,128)(2,1)} copy(bf16[4,8,8,8,512]{4,3,2,1,0:T(8,128)(2,1)} %bitcast.18) | data formatting | bytes 4194304 | tf_op jit(solution)/shard_map/reshape | solution.py:290
  4.4 0.0 copy-start.1
  4.4 0.0 copy-start.2
  4.4 0.0 copy-start.8
  4.4 64.8 %shard_map.82.frame = bf16[6,10,64,512]{3,2,1,0:T(8,128)(2,1)} custom-call(bf16[4,8,64,512]{3,2,1,0:T(8,128)(2,1)} %bitcast.17), custom_call_target="tpu_custom_call" | custom-call | tf_op jit(solution)/shard_map/pallas_call | solution.py:292
  69.2 0.1 fusion.2
  69.3 0.1 stack.50
  69.4 0.1 stack.51
  69.5 0.1 stack.52
  69.5 0.1 stack.53
  69.6 0.1 stack.54
  69.7 0.1 stack.55
  69.8 0.1 stack.56
  69.9 0.1 stack.57
  70.0 0.1 stack.58
  70.1 0.1 stack.59
  70.1 0.1 copy.17
  70.2 0.1 broadcast_in_dim.24
  70.4 0.1 broadcast_in_dim.28.bias
  70.5 0.0 copy-done.1
  70.5 0.0 copy-done.2
  70.5 0.0 copy-done.8
  70.5 32.2 %shard_map.83 = (bf16[32,64,512]{2,1,0:T(8,128)(2,1)}, bf16[2,256,512]{2,1,0:T(8,128)(2,1)S(1)}) custom-call(s32[6,10]{1,0:T(8,128)S(1)} %get-tuple-element.17.ok_ref, bf16[6,10,64,512]{3,2,1,0:T(8,128)(2,1)} %shard_map.82.frame, f32[1,512]{1,0:T(1,128)S(1)} %bitcast.14, bf16[512,1536]{1,0:T(8,128)(2,1)S(1)} %copy-done.1, bf16[512,512]{1,0:T(8,128)(2,1)S(1)} %copy-done.2, ...), custom_call_target="tpu_custom_call" | custom-call | tf_op jit(solution)/shard_map/pallas_call | solution.py:308
  102.7 0.0 copy-start.3
  102.7 0.8 copy-done.3
  103.5 0.0 copy-start.11
  103.5 0.0 copy-start
  103.5 0.0 copy-start.9
  103.5 0.0 copy-start.10
  103.5 14.7 %shard_map.84 = (bf16[3,64,512]{2,1,0:T(8,128)(2,1)}, bf16[3,64,512]{2,1,0:T(8,128)(2,1)}, bf16[2,256,512]{2,1,0:T(8,128)(2,1)}, bf16[4,32,512]{2,1,0:T(8,128)(2,1)}) custom-call(bf16[32,64,512]{2,1,0:T(8,128)(2,1)} %get-tuple-element.11.mixed, bf16[2,256,512]{2,1,0:T(8,128)(2,1)} %copy-done.3), custom_call_target="tpu_custom_call" | custom-call | tf_op jit(solution)/shard_map/pallas_call | solution.py:325
  118.3 0.0 copy-done.11
  118.3 0.1 broadcast_in_dim.27.weight
  118.4 0.0 copy-done
  118.4 0.0 copy-done.9
  118.4 0.0 copy-done.10
  118.4 0.0 copy-start.4
  118.4 1.0 copy-done.4
  119.5 0.0 copy-start.5
  119.5 0.9 copy-done.5
  120.4 0.9 copy-done.6
  121.3 0.0 copy-start.7
  121.3 0.9 copy-done.7
  122.2 56.3 %shard_map.85 = bf16[32,64,512]{2,1,0:T(8,128)(2,1)} custom-call(s32[4]{0:T(128)S(1)} %add_convert_fusion.flags, bf16[32,64,512]{2,1,0:T(8,128)(2,1)S(1)} %copy-done, bf16[3,64,512]{2,1,0:T(8,128)(2,1)S(1)} %copy-done.5, bf16[3,64,512]{2,1,0:T(8,128)(2,1)S(1)} %copy-done.6, bf16[2,256,512]{2,1,0:T(8,128)(2,1)S(1)} %copy-done.4, ...), custom_call_target="tpu_custom_call" | custom-call | tf_op jit(solution)/shard_map/pallas_call | solution.py:341
  (4 shorter events, 0.0 us)
Async XLA Ops:
  4.4 66.1 %copy-start.1 = (bf16[512,1536]{1,0:T(8,128)(2,1)S(1)}, bf16[512,1536]{1,0:T(8,128)(2,1)}, u32[]{:S(2)}) copy-start(bf16[512,1536]{1,0:T(8,128)(2,1)} %w_qkv.1) | copy-start | bytes 4718596
  4.4 66.1 %copy-start.2 = (bf16[512,512]{1,0:T(8,128)(2,1)S(1)}, bf16[512,512]{1,0:T(8,128)(2,1)}, u32[]{:S(2)}) copy-start(bf16[512,512]{1,0:T(8,128)(2,1)} %w_out.1) | copy-start | bytes 1572868
  4.4 66.1 %copy-start.8 = (f32[512]{0:T(512)S(1)}, f32[512]{0:T(512)}, u32[]{:S(2)}) copy-start(f32[512]{0:T(512)} %param.10) | copy-start | bytes 6148
  102.7 0.8 copy-start.3
  103.5 14.7 %copy-start.11 = (f32[7,7,512]{2,1,0:T(8,128)S(1)}, f32[7,7,512]{2,1,0:T(8,128)}, u32[]{:S(2)}) copy-start(f32[7,7,512]{2,1,0:T(8,128)} %param.13) | copy-start | bytes 301060
  103.5 14.9 %copy-start = (bf16[32,64,512]{2,1,0:T(8,128)(2,1)S(1)}, bf16[32,64,512]{2,1,0:T(8,128)(2,1)}, u32[]{:S(2)}) copy-start(bf16[32,64,512]{2,1,0:T(8,128)(2,1)} %get-tuple-element.11.mixed) | copy-start | bytes 6291460
  103.5 14.9 %copy-start.9 = (f32[512]{0:T(512)S(1)}, f32[512]{0:T(512)}, u32[]{:S(2)}) copy-start(f32[512]{0:T(512)} %param.14) | copy-start | bytes 6148
  103.5 14.9 %copy-start.10 = (f32[512]{0:T(512)S(1)}, f32[512]{0:T(512)}, u32[]{:S(2)}) copy-start(f32[512]{0:T(512)} %param.15) | copy-start | bytes 6148
  118.4 1.0 copy-start.4
  119.5 0.9 copy-start.5
  120.4 0.9 copy-start.6
  121.3 0.9 copy-start.7

commit v2 on v1

--- a/solution.py
+++ b/solution.py
@@ -86,7 +86,7 @@
     return finish
 
 
-def token_halo_kernel(sizes, blocks, frame, send_sems, recv_sems, own_sem):
+def token_halo_kernel(sizes, blocks, frame, send_sems, recv_sems):
     def span(step, n):
         if step == -1:
             return pl.ds(0, 1), pl.ds(n + 1, 1)
@@ -98,11 +98,7 @@
         (sr, tr), (sc, tc) = span(dr, BR), span(dc, BC)
         return blocks.at[sr, sc], frame.at[tr, tc]
 
-    own = pltpu.make_async_copy(blocks, frame.at[pl.ds(1, BR), pl.ds(1, BC)], own_sem)
-    own.start()
-    finish = exchange(sizes, views, send_sems, recv_sems)
-    own.wait()
-    finish()
+    exchange(sizes, views, send_sems, recv_sems)()
 
 
 def mixed_halo_kernel(
@@ -127,28 +123,47 @@
 
 
 def attention_kernel(
-    ok_ref, frame, gain, w_qkv, w_out, bias, mixed, edges, qkv, normed, att, mix
+    ok_ref, blocks, frame, gain, w_qkv, w_out, bias, mixed, edges, qkv, normed, att, mix
 ):
     width = frame.shape[-1]
     tok = BLK * BLK
     half = width // 2
     head = width // HEADS
 
-    def project(i, carry):
-        for j in range(BC + 2):
-            x = frame[i, j].astype(jnp.float32)
-            x = jnp.where(ok_ref[i, j] != 0, x, 0.0)
-            cent = x - jnp.mean(x, axis=-1, keepdims=True)
-            var = jnp.mean(cent * cent, axis=-1, keepdims=True)
-            y = cent * lax.rsqrt(var + 1e-06) * gain[...]
-            normed[pl.ds(j * tok, tok), :] = y.astype(jnp.bfloat16)
+    def norm(x, at):
+        cent = x - jnp.mean(x, axis=-1, keepdims=True)
+        var = jnp.mean(cent * cent, axis=-1, keepdims=True)
+        y = cent * lax.rsqrt(var + 1e-06) * gain[...]
+        normed[pl.ds(at * tok, tok), :] = y.astype(jnp.bfloat16)
+
+    def halo(i, j):
+        x = frame[i, j].astype(jnp.float32)
+        return jnp.where(ok_ref[i, j] != 0, x, 0.0)
+
+    def own_row(i, carry):
+        for j in range(BC):
+            norm(blocks[i, j].astype(jnp.float32), j + 1)
+        norm(halo(i + 1, 0), 0)
+        norm(halo(i + 1, BC + 1), BC + 1)
         for n in range(3):
             cols = pl.ds(n * width, width)
             p = jnp.dot(normed[...], w_qkv[:, cols], preferred_element_type=jnp.float32)
+            qkv[i + 1, :, :, cols] = p.astype(jnp.bfloat16).reshape(BC + 2, tok, width)
+        return carry
+
+    lax.fori_loop(0, BR, own_row, 0)
+
+    def halo_row(t, carry):
+        i = t * (BR + 1)
+        for j in range(BC + 2):
+            norm(halo(i, j), j)
+        for n in (1, 2):
+            cols = pl.ds(n * width, width)
+            p = jnp.dot(normed[...], w_qkv[:, cols], preferred_element_type=jnp.float32)
             qkv[i, :, :, cols] = p.astype(jnp.bfloat16).reshape(BC + 2, tok, width)
         return carry
 
-    lax.fori_loop(0, BR + 2, project, 0)
+    lax.fori_loop(0, 2, halo_row, 0)
 
     shape = (GROUP * tok, half)
     same = (
@@ -211,7 +226,7 @@
         d = jnp.dot(a, w_out[...], preferred_element_type=jnp.float32)
         rows = pl.ds(bi * BLK, BLK)
         for bj in range(BC):
-            m = frame[bi + 1, bj + 1].astype(jnp.float32) + d[bj * tok : (bj + 1) * tok]
+            m = blocks[bi, bj].astype(jnp.float32) + d[bj * tok : (bj + 1) * tok]
             mix[rows, pl.ds(bj * BLK, BLK), :] = m.reshape(BLK, BLK, width)
         mixed[rows] = mix[rows].astype(jnp.bfloat16)
         for side, start in ((0, 0), (1, (BC - 1) * BLK)):
@@ -228,45 +243,48 @@
     height, breadth, width = mixed.shape
     up, down, left, right = [flags[k] != 0 for k in range(4)]
     f32 = jnp.float32
+    chunks = width // 128
+
+    def put(rows, cols, v):
+        for l in range(chunks):
+            framed[l, rows, cols, :] = v[..., l * 128 : (l + 1) * 128]
 
     def fill(i, carry):
         rows = pl.ds(i * BLK, BLK)
-        framed[pl.ds(i * BLK + 3, BLK), pl.ds(8, breadth), :] = mixed[rows].astype(f32)
+        into = pl.ds(i * BLK + 3, BLK)
+        put(into, pl.ds(8, breadth), mixed[rows].astype(f32))
         for k, ok, start in ((0, left, 0), (1, right, breadth + 8)):
             v = sides[k, pl.ds(i * BLK * 8, BLK * 8), :].astype(f32)
-            framed[pl.ds(i * BLK + 3, BLK), pl.ds(start, 8), :] = jnp.where(ok, v, 0.0).reshape(
-                BLK, 8, width
-            )
+            put(into, pl.ds(start, 8), jnp.where(ok, v, 0.0).reshape(BLK, 8, width))
         return carry
 
     lax.fori_loop(0, height // BLK, fill, 0)
     for k, ok, ref, start in ((0, up, top, 0), (2, down, bottom, height + 3)):
         rows = pl.ds(start, 3)
-        framed[rows, pl.ds(8, breadth), :] = jnp.where(ok, ref[...].astype(f32), 0.0)
+        put(rows, pl.ds(8, breadth), jnp.where(ok, ref[...].astype(f32), 0.0))
         for h, side_ok, col in ((0, left, 0), (1, right, breadth + 8)):
             v = corners[k + h].astype(f32).reshape(4, 8, width)
             v = v[1:] if k == 0 else v[:3]
             both = jnp.logical_and(ok, side_ok)
-            framed[rows, pl.ds(col, 8), :] = jnp.where(both, v, 0.0)
+            put(rows, pl.ds(col, 8), jnp.where(both, v, 0.0))
 
     def row_block(i, carry):
         r0 = i * BLK
 
         def lanes(l, inner):
-            lane = pl.ds(pl.multiple_of(l * 128, 128), 128)
             for c0 in range(0, breadth, 8):
-                acc = jnp.zeros((BLK, 8, 128), f32) + bias[:, lane]
+                acc = jnp.zeros((BLK, 8, 128), f32) + bias[l]
                 for dx in range(7):
-                    v = framed[pl.ds(r0, BLK + 6), pl.ds(c0 + dx + 5, 8), lane]
+                    v = framed[l, pl.ds(r0, BLK + 6), pl.ds(c0 + dx + 5, 8), :]
                     for dy in range(7):
-                        acc = acc + v[dy : dy + BLK] * weight[dy * 7 + dx, :, lane]
-                filt[:, pl.ds(c0, 8), lane] = acc
+                        acc = acc + v[dy : dy + BLK] * weight[l, dy * 7 + dx]
+                filt[l, :, pl.ds(c0, 8), :] = acc
             return inner
 
-        lax.fori_loop(0, width // 128, lanes, 0)
+        lax.fori_loop(0, chunks, lanes, 0)
 
         def norm(y, inner):
-            f = filt[y]
+            f = jnp.concatenate([filt[l, y] for l in range(chunks)], axis=-1)
             cent = f - jnp.mean(f, axis=-1, keepdims=True)
             var = jnp.mean(cent * cent, axis=-1, keepdims=True)
             branch = cent * lax.rsqrt(var + 1e-06) * gain[...]
@@ -294,7 +312,7 @@
         out_shape=jax.ShapeDtypeStruct((BR + 2, BC + 2, tok, width), bf16),
         in_specs=[ANY],
         out_specs=ANY,
-        scratch_shapes=[dma((8,)), dma((8,)), dma],
+        scratch_shapes=[dma((8,)), dma((8,))],
         compiler_params=pltpu.CompilerParams(collective_id=0, has_side_effects=True),
     )(blocks)
 
@@ -311,7 +329,7 @@
             jax.ShapeDtypeStruct((height, breadth, width), bf16),
             jax.ShapeDtypeStruct((2, height * 8, width), bf16),
         ),
-        in_specs=[SM, VM, VM, VM, VM, VM],
+        in_specs=[SM] + [VM] * 6,
         out_specs=(VM, VM),
         scratch_shapes=[
             pltpu.VMEM((BR + 2, BC + 2, tok, 3 * width), bf16),
@@ -320,7 +338,7 @@
             pltpu.VMEM((height, breadth, width), f32),
         ],
         compiler_params=pltpu.CompilerParams(vmem_limit_bytes=50 * MIB),
-    )(near.astype(jnp.int32), frame, ln_gain.reshape(1, width), w_qkv, w_out, bias)
+    )(near.astype(jnp.int32), blocks, frame, ln_gain.reshape(1, width), w_qkv, w_out, bias)
 
     top, bottom, sides, corners = pl.pallas_call(
         functools.partial(mixed_halo_kernel, sizes),
@@ -337,15 +355,17 @@
     )(mixed, edges)
 
     flags = jnp.stack([row > 0, row < sizes[0] - 1, col > 0, col < sizes[1] - 1])
-    weight = jnp.broadcast_to(conv_weight.reshape(49, 1, width), (49, 8, width))
+    chunks = width // 128
+    weight = conv_weight.reshape(49, chunks, 1, 128).transpose(1, 0, 2, 3)
+    weight = jnp.broadcast_to(weight, (chunks, 49, 8, 128))
     return pl.pallas_call(
         conv_kernel,
         out_shape=jax.ShapeDtypeStruct((height, breadth, width), bf16),
         in_specs=[SM] + [VM] * 8,
         out_specs=VM,
         scratch_shapes=[
-            pltpu.VMEM((height + 6, breadth + 16, width), f32),
-            pltpu.VMEM((BLK, breadth, width), f32),
+            pltpu.VMEM((width // 128, height + 6, breadth + 16, 128), f32),
+            pltpu.VMEM((width // 128, BLK, breadth, 128), f32),
         ],
         compiler_params=pltpu.CompilerParams(vmem_limit_bytes=40 * MIB),
     )(
@@ -356,7 +376,7 @@
         sides,
         corners,
         weight,
-        conv_bias.reshape(1, width),
+        conv_bias.reshape(chunks, 1, 128),
         conv_gain.reshape(1, width),
     )
 

time: 180 us -> 102 us (0.57)
  Pallas kernels: 168 us -> 91.5 us
    pallas_call x1, Pallas kernels: 64.8 us -> 19 us  [per_device(): pl.pallas_call(functools.partial(token_halo_kernel, sizes), out_shape=jax...]
    pallas_call x1, Pallas kernels: 56.3 us -> 25.5 us  [per_device(): pl.pallas_call(conv_kernel, out_shape=jax.ShapeDtypeStruct((height, bread...]
where the time goes in v2:
time: 102 us
  Pallas kernels  91.5 us (90%)
  local copies, waits for them, and re-layouts  9.36 us (9%)
    pallas_call x1, Pallas kernels, per_device(): pl.pallas_call(attention_kernel, out_shape=(jax.ShapeDtypeStruct((height,...  30.5 us
    pallas_call x1, Pallas kernels, per_device(): pl.pallas_call(conv_kernel, out_shape=jax.ShapeDtypeStruct((height, bread...  25.5 us
    pallas_call x1, Pallas kernels, per_device(): pl.pallas_call(functools.partial(token_halo_kernel, sizes), out_shape=jax...  19 us
    pallas_call x1, Pallas kernels, per_device(): pl.pallas_call(functools.partial(mixed_halo_kernel, sizes), out_shape=(ja...  16.5 us
    unnamed x24, local copies, waits for them, and re-layouts  4.61 us
    reshape x1, local copies, waits for them, and re-layouts, per_device(): blocks = tokens.reshape(BR, BLK, BC, BLK, width).transpose(0, 2, 1, 3, 4)  3.2 us

profile of v2, /device:TPU:1, one launch (start us, length us, event | category | flops | bytes accessed | tf_op | source)
XLA Modules:
  0.0 102.0 jit_solution(2635317702676387573)
XLA Ops:
  0.0 0.1 add_convert_fusion.flags
  0.1 0.8 fusion
  0.9 0.1 reshape.87
  1.0 0.1 reshape.88
  1.1 0.1 fusion.1
  1.2 3.2 %copy.24 = bf16[4,8,8,8,512]{4,3,1,2,0:T(8,128)(2,1)} copy(bf16[4,8,8,8,512]{4,3,2,1,0:T(8,128)(2,1)} %bitcast.24) | data formatting | bytes 4194304 | tf_op jit(solution)/shard_map/reshape | solution.py:308
  4.4 0.0 copy-start.1
  4.4 0.0 copy-start.2
  4.4 0.0 copy-start.10
  4.4 19.0 %shard_map.82.frame = bf16[6,10,64,512]{3,2,1,0:T(8,128)(2,1)} custom-call(bf16[4,8,64,512]{3,2,1,0:T(8,128)(2,1)} %bitcast.22), custom_call_target="tpu_custom_call" | custom-call | tf_op jit(solution)/shard_map/pallas_call | solution.py:310
  23.4 0.1 fusion.2
  23.5 0.1 stack.50
  23.6 0.1 stack.51
  23.7 0.1 stack.52
  23.8 0.1 stack.53
  23.9 0.1 stack.54
  23.9 0.1 stack.55
  24.0 0.1 stack.56
  24.1 0.1 stack.57
  24.2 0.1 stack.58
  24.3 0.1 stack.59
  24.4 0.1 copy.19
  24.4 0.1 broadcast_in_dim.24
  24.6 0.1 broadcast_in_dim.28.bias
  24.7 0.0 copy-done.1
  24.7 0.0 copy-done.2
  24.7 0.0 copy-done.10
  24.8 30.5 %shard_map.83 = (bf16[32,64,512]{2,1,0:T(8,128)(2,1)}, bf16[2,256,512]{2,1,0:T(8,128)(2,1)S(1)}) custom-call(s32[6,10]{1,0:T(8,128)S(1)} %get-tuple-element.17.ok_ref, bf16[4,8,64,512]{3,2,1,0:T(8,128)(2,1)} %bitcast.23, bf16[6,10,64,512]{3,2,1,0:T(8,128)(2,1)} %shard_map.82.frame, f32[1,512]{1,0:T(1,128)S(1)} %bitcast.21, bf16[512,1536]{1,0:T(8,128)(2,1)S(1)} %copy-done.1, ...), custom_call_target="tpu_custom_call" | custom-call | tf_op jit(solution)/shard_map/pallas_call | solution.py:326
  55.3 0.0 copy-start.3
  55.3 0.8 copy-done.3
  56.1 0.0 copy-start
  56.1 0.0 copy-start.8
  56.1 0.0 copy-start.9
  56.1 16.5 %shard_map.84 = (bf16[3,64,512]{2,1,0:T(8,128)(2,1)}, bf16[3,64,512]{2,1,0:T(8,128)(2,1)}, bf16[2,256,512]{2,1,0:T(8,128)(2,1)}, bf16[4,32,512]{2,1,0:T(8,128)(2,1)}) custom-call(bf16[32,64,512]{2,1,0:T(8,128)(2,1)} %get-tuple-element.11.mixed, bf16[2,256,512]{2,1,0:T(8,128)(2,1)} %copy-done.3), custom_call_target="tpu_custom_call" | custom-call | tf_op jit(solution)/shard_map/pallas_call | solution.py:343
  72.6 0.0 copy-done.11
  72.6 0.1 broadcast_in_dim.27.weight
  72.7 0.0 copy-done
  72.7 0.0 copy-done.8
  72.7 0.0 copy-done.9
  72.7 0.0 copy-start.4
  72.7 1.0 %copy-done.4 = bf16[2,256,512]{2,1,0:T(8,128)(2,1)S(1)} copy-done((bf16[2,256,512]{2,1,0:T(8,128)(2,1)S(1)}, bf16[2,256,512]{2,1,0:T(8,128)(2,1)}, u32[]{:S(2)}) %copy-start.4) | copy-done | bytes 524312
  73.8 0.0 copy-start.5
  73.8 0.9 copy-done.5
  74.7 0.0 copy-start.6
  74.7 0.9 copy-done.6
  75.6 0.0 copy-start.7
  75.6 0.9 copy-done.7
  76.5 25.5 %shard_map.85 = bf16[32,64,512]{2,1,0:T(8,128)(2,1)} custom-call(s32[4]{0:T(128)S(1)} %add_convert_fusion.flags, bf16[32,64,512]{2,1,0:T(8,128)(2,1)S(1)} %copy-done, bf16[3,64,512]{2,1,0:T(8,128)(2,1)S(1)} %copy-done.5, bf16[3,64,512]{2,1,0:T(8,128)(2,1)S(1)} %copy-done.6, bf16[2,256,512]{2,1,0:T(8,128)(2,1)S(1)} %copy-done.4, ...), custom_call_target="tpu_custom_call" | custom-call | tf_op jit(solution)/shard_map/pallas_call | solution.py:361
  (5 shorter events, 0.1 us)
Async XLA Ops:
  4.4 20.3 %copy-start.1 = (bf16[512,1536]{1,0:T(8,128)(2,1)S(1)}, bf16[512,1536]{1,0:T(8,128)(2,1)}, u32[]{:S(2)}) copy-start(bf16[512,1536]{1,0:T(8,128)(2,1)} %w_qkv.1) | copy-start | bytes 4718596
  4.4 20.3 %copy-start.2 = (bf16[512,512]{1,0:T(8,128)(2,1)S(1)}, bf16[512,512]{1,0:T(8,128)(2,1)}, u32[]{:S(2)}) copy-start(bf16[512,512]{1,0:T(8,128)(2,1)} %w_out.1) | copy-start | bytes 1572868
  4.4 20.3 %copy-start.10 = (f32[512]{0:T(512)S(1)}, f32[512]{0:T(512)}, u32[]{:S(2)}) copy-start(f32[512]{0:T(512)} %param.10) | copy-start | bytes 6148
  55.3 0.8 copy-start.3
  56.1 16.5 %copy-start.11 = (f32[7,7,512]{2,1,0:T(8,128)S(1)}, f32[7,7,512]{2,1,0:T(8,128)}, u32[]{:S(2)}) copy-start(f32[7,7,512]{2,1,0:T(8,128)} %param.13) | copy-start | bytes 301060
  56.1 16.6 %copy-start = (bf16[32,64,512]{2,1,0:T(8,128)(2,1)S(1)}, bf16[32,64,512]{2,1,0:T(8,128)(2,1)}, u32[]{:S(2)}) copy-start(bf16[32,64,512]{2,1,0:T(8,128)(2,1)} %get-tuple-element.11.mixed) | copy-start | bytes 6291460
  56.1 16.6 %copy-start.8 = (f32[512]{0:T(512)S(1)}, f32[512]{0:T(512)}, u32[]{:S(2)}) copy-start(f32[512]{0:T(512)} %param.14) | copy-start | bytes 6148
  56.1 16.6 %copy-start.9 = (f32[512]{0:T(512)S(1)}, f32[512]{0:T(512)}, u32[]{:S(2)}) copy-start(f32[512]{0:T(512)} %param.15) | copy-start | bytes 6148
  72.7 1.0 %copy-start.4 = (bf16[2,256,512]{2,1,0:T(8,128)(2,1)S(1)}, bf16[2,256,512]{2,1,0:T(8,128)(2,1)}, u32[]{:S(2)}) copy-start(bf16[2,256,512]{2,1,0:T(8,128)(2,1)} %get-tuple-element.15.sides) | copy-start | bytes 1572868
  73.8 0.9 copy-start.5
  74.7 0.9 copy-start.6
  75.6 0.9 copy-start.7

commit v3 on v2

--- a/solution.py
+++ b/solution.py
@@ -26,10 +26,9 @@
     return hits.reshape(tiles_r * BR, tiles_c * BC)
 
 
-def exchange(sizes, views, send_sems, recv_sems):
+def exchange(sizes, views, send_sems, recv_sems, greet):
     n_r, n_c = sizes
     r, c = lax.axis_index("row"), lax.axis_index("col")
-    barrier = pltpu.get_barrier_semaphore()
 
     def there(dr, dc):
         ok = None
@@ -46,15 +45,17 @@
     def target(dr, dc):
         return {"row": r + dr, "col": c + dc}
 
-    for dr, dc in SIDES:
-        @pl.when(there(dr, dc))
-        def _():
-            pl.semaphore_signal(
-                barrier, inc=1, device_id=target(dr, dc), device_id_type=pl.DeviceIdType.MESH
-            )
-
-    peers = sum(there(dr, dc).astype(jnp.int32) for dr, dc in SIDES)
-    pl.semaphore_wait(barrier, peers)
+    if greet:
+        barrier = pltpu.get_barrier_semaphore()
+        for dr, dc in SIDES:
+            @pl.when(there(dr, dc))
+            def _():
+                pl.semaphore_signal(
+                    barrier, inc=1, device_id=target(dr, dc), device_id_type=pl.DeviceIdType.MESH
+                )
+
+        peers = sum(there(dr, dc).astype(jnp.int32) for dr, dc in SIDES)
+        pl.semaphore_wait(barrier, peers)
 
     def copy(k):
         dr, dc = SIDES[k]
@@ -86,7 +87,7 @@
     return finish
 
 
-def token_halo_kernel(sizes, blocks, frame, send_sems, recv_sems):
+def token_views(blocks, frame):
     def span(step, n):
         if step == -1:
             return pl.ds(0, 1), pl.ds(n + 1, 1)
@@ -98,12 +99,10 @@
         (sr, tr), (sc, tc) = span(dr, BR), span(dc, BC)
         return blocks.at[sr, sc], frame.at[tr, tc]
 
-    exchange(sizes, views, send_sems, recv_sems)()
-
-
-def mixed_halo_kernel(
-    sizes, mixed, edges, top, bottom, sides, corners, send_sems, recv_sems
-):
+    return views
+
+
+def mixed_views(mixed, edges, top, bottom, sides, corners):
     height = mixed.shape[0]
     tall = edges.shape[1]
 
@@ -119,12 +118,34 @@
         place = (2 if dr == -1 else 0) + 1 - mine
         return edges.at[mine, rows], corners.at[place]
 
-    exchange(sizes, views, send_sems, recv_sems)()
+    return views
 
 
 def attention_kernel(
-    ok_ref, blocks, frame, gain, w_qkv, w_out, bias, mixed, edges, qkv, normed, att, mix
+    sizes,
+    ok_ref,
+    blocks,
+    gain,
+    w_qkv,
+    w_out,
+    bias,
+    mixed,
+    top,
+    bottom,
+    sides,
+    corners,
+    edges,
+    frame,
+    qkv,
+    normed,
+    att,
+    mix,
+    send_a,
+    recv_a,
+    send_b,
+    recv_b,
 ):
+    landed = exchange(sizes, token_views(blocks, frame), send_a, recv_a, True)
     width = frame.shape[-1]
     tok = BLK * BLK
     half = width // 2
@@ -140,30 +161,44 @@
         x = frame[i, j].astype(jnp.float32)
         return jnp.where(ok_ref[i, j] != 0, x, 0.0)
 
+    def dots(i, at, cols_at, count, parts):
+        rows = pl.ds(at * tok, count * tok)
+        for n in parts:
+            cols = pl.ds(n * width, width)
+            p = jnp.dot(normed[rows, :], w_qkv[:, cols], preferred_element_type=jnp.float32)
+            qkv[i, pl.ds(cols_at, count), :, cols] = p.astype(jnp.bfloat16).reshape(
+                count, tok, width
+            )
+
     def own_row(i, carry):
         for j in range(BC):
-            norm(blocks[i, j].astype(jnp.float32), j + 1)
-        norm(halo(i + 1, 0), 0)
-        norm(halo(i + 1, BC + 1), BC + 1)
-        for n in range(3):
-            cols = pl.ds(n * width, width)
-            p = jnp.dot(normed[...], w_qkv[:, cols], preferred_element_type=jnp.float32)
-            qkv[i + 1, :, :, cols] = p.astype(jnp.bfloat16).reshape(BC + 2, tok, width)
+            norm(blocks[i, j].astype(jnp.float32), j)
+        dots(i + 1, 0, 1, BC, range(3))
         return carry
-
-    lax.fori_loop(0, BR, own_row, 0)
 
     def halo_row(t, carry):
         i = t * (BR + 1)
         for j in range(BC + 2):
             norm(halo(i, j), j)
+        dots(i, 0, 0, BC + 2, (1, 2))
+        return carry
+
+    def halo_columns():
+        for t in range(2):
+            j = t * (BC + 1)
+            for i in range(BR):
+                norm(halo(i + 1, j), t * BR + i)
         for n in (1, 2):
             cols = pl.ds(n * width, width)
-            p = jnp.dot(normed[...], w_qkv[:, cols], preferred_element_type=jnp.float32)
-            qkv[i, :, :, cols] = p.astype(jnp.bfloat16).reshape(BC + 2, tok, width)
-        return carry
-
-    lax.fori_loop(0, 2, halo_row, 0)
+            p = jnp.dot(
+                normed[pl.ds(0, 2 * BR * tok), :],
+                w_qkv[:, cols],
+                preferred_element_type=jnp.float32,
+            ).astype(jnp.bfloat16)
+            for t in range(2):
+                for i in range(BR):
+                    k = (t * BR + i) * tok
+                    qkv[i + 1, t * (BC + 1), :, cols] = p[k : k + tok]
 
     shape = (GROUP * tok, half)
     same = (
@@ -171,70 +206,87 @@
         == lax.broadcasted_iota(jnp.int32, shape, 1) // head
     )
 
-    def attend(b, carry):
-        bi = b // BC
-        bj = b % BC
+    def attend(bi, bj):
+        b = bi * BC + bj
         ok = ok_ref[bi + 1, bj + 1] != 0
-
-        @pl.when(ok)
-        def _():
-            for g in range(2):
-                q = qkv[bi + 1, bj + 1, :, pl.ds(g * half, half)].astype(jnp.float32)
-                q = q * head ** (-0.5)
-                q = jnp.where(same, jnp.concatenate([q] * GROUP, axis=0), 0.0)
-                q = q.astype(jnp.bfloat16)
-
-                def window(start):
-                    return jnp.concatenate(
-                        [
-                            qkv[bi + a, pl.ds(bj, 3), :, pl.ds(start, half)].reshape(
-                                3 * tok, half
-                            )
-                            for a in range(3)
-                        ],
-                        axis=0,
-                    )
-
-                s = lax.dot_general(
-                    q,
-                    window(width + g * half),
-                    (((1,), (1,)), ((), ())),
-                    preferred_element_type=jnp.float32,
+        for g in range(2):
+            q = qkv[bi + 1, bj + 1, :, pl.ds(g * half, half)].astype(jnp.float32)
+            q = q * head ** (-0.5)
+            q = jnp.where(same, jnp.concatenate([q] * GROUP, axis=0), 0.0)
+            q = q.astype(jnp.bfloat16)
+
+            def window(start):
+                return jnp.concatenate(
+                    [
+                        qkv[bi + a, pl.ds(bj, 3), :, pl.ds(start, half)].reshape(
+                            3 * tok, half
+                        )
+                        for a in range(3)
+                    ],
+                    axis=0,
                 )
-                s = s + bias[b]
-                e = jnp.exp(s - jnp.max(s, axis=-1, keepdims=True))
-                total = jnp.sum(e, axis=-1, keepdims=True)
-                o = jnp.dot(
-                    e.astype(jnp.bfloat16),
-                    window(2 * width + g * half),
-                    preferred_element_type=jnp.float32,
-                )
-                o = jnp.where(same, o * (1.0 / total), 0.0)
-                o = o[:tok] + o[tok : 2 * tok] + o[2 * tok : 3 * tok] + o[3 * tok :]
-                att[b, :, pl.ds(g * half, half)] = o.astype(jnp.bfloat16)
-
-        @pl.when(jnp.logical_not(ok))
-        def _():
-            att[b] = jnp.zeros((tok, width), jnp.bfloat16)
-
-        return carry
-
-    lax.fori_loop(0, BR * BC, attend, 0)
-
-    def out(bi, carry):
-        a = att[pl.ds(bi * BC, BC)].reshape(BC * tok, width)
+
+            s = lax.dot_general(
+                q,
+                window(width + g * half),
+                (((1,), (1,)), ((), ())),
+                preferred_element_type=jnp.float32,
+            )
+            s = s + bias[b]
+            e = jnp.exp(s - jnp.max(s, axis=-1, keepdims=True))
+            total = jnp.sum(e, axis=-1, keepdims=True)
+            o = jnp.dot(
+                e.astype(jnp.bfloat16),
+                window(2 * width + g * half),
+                preferred_element_type=jnp.float32,
+            )
+            o = jnp.where(same, o * (1.0 / total), 0.0)
+            o = o[:tok] + o[tok : 2 * tok] + o[2 * tok : 3 * tok] + o[3 * tok :]
+            o = jnp.where(ok, o, 0.0)
+            att[b, :, pl.ds(g * half, half)] = o.astype(jnp.bfloat16)
+
+    def loop(count, place):
+        def step(t, carry):
+            attend(*place(t))
+            return carry
+
+        lax.fori_loop(0, count, step, 0)
+
+    def add(places):
+        a = jnp.concatenate([att[bi * BC + bj] for bi, bj in places], axis=0)
         d = jnp.dot(a, w_out[...], preferred_element_type=jnp.float32)
+        for n, (bi, bj) in enumerate(places):
+            m = blocks[bi, bj].astype(jnp.float32) + d[n * tok : (n + 1) * tok]
+            rows, cols = pl.ds(bi * BLK, BLK), pl.ds(bj * BLK, BLK)
+            mix[rows, cols, :] = m.reshape(BLK, BLK, width)
+            if bj in (0, BC - 1):
+                edges[min(bj, 1), pl.ds(bi * tok, tok), :] = m.astype(jnp.bfloat16)
+
+    def write(bi):
         rows = pl.ds(bi * BLK, BLK)
-        for bj in range(BC):
-            m = blocks[bi, bj].astype(jnp.float32) + d[bj * tok : (bj + 1) * tok]
-            mix[rows, pl.ds(bj * BLK, BLK), :] = m.reshape(BLK, BLK, width)
         mixed[rows] = mix[rows].astype(jnp.bfloat16)
-        for side, start in ((0, 0), (1, (BC - 1) * BLK)):
-            m = mix[rows, pl.ds(start, BLK), :].reshape(tok, width)
-            edges[side, pl.ds(bi * tok, tok), :] = m.astype(jnp.bfloat16)
-        return carry
-
-    lax.fori_loop(0, BR, out, 0)
+
+    inner = BC - 2
+    lax.fori_loop(0, BR, own_row, 0)
+    loop(inner, lambda t: (1, 1 + t))
+    landed()
+    lax.fori_loop(0, 2, halo_row, 0)
+    halo_columns()
+    loop(BC, lambda t: (0, t))
+    loop(BC, lambda t: (BR - 1, t))
+    loop(2 * (BR - 2), lambda t: (1 + t // 2, (t % 2) * (BC - 1)))
+    add([(0, j) for j in range(BC)])
+    add([(BR - 1, j) for j in range(BC)])
+    add([(i, j) for i in range(1, BR - 1) for j in (0, BC - 1)])
+    write(0)
+    write(BR - 1)
+    views = mixed_views(mixed, edges, top, bottom, sides, corners)
+    landed = exchange(sizes, views, send_b, recv_b, False)
+    loop(inner * (BR - 3), lambda t: (2 + t // inner, 1 + t % inner))
+    add([(i, j) for i in range(1, BR - 1) for j in range(1, BC - 1)])
+    for i in range(1, BR - 1):
+        write(i)
+    landed()
 
 
 def conv_kernel(
@@ -307,15 +359,6 @@
 
     blocks = tokens.reshape(BR, BLK, BC, BLK, width).transpose(0, 2, 1, 3, 4)
     blocks = blocks.reshape(BR, BC, tok, width)
-    frame = pl.pallas_call(
-        functools.partial(token_halo_kernel, sizes),
-        out_shape=jax.ShapeDtypeStruct((BR + 2, BC + 2, tok, width), bf16),
-        in_specs=[ANY],
-        out_specs=ANY,
-        scratch_shapes=[dma((8,)), dma((8,))],
-        compiler_params=pltpu.CompilerParams(collective_id=0, has_side_effects=True),
-    )(blocks)
-
     table = jnp.pad(block_table(tissue_list), 1)
     near = lax.dynamic_slice(table, (row * BR, col * BC), (BR + 2, BC + 2))
     okay = jnp.stack(
@@ -323,36 +366,33 @@
     ).reshape(BR * BC, 1, 9)
     bias = jnp.repeat(jnp.where(okay, 0.0, -1e30).astype(f32), tok, axis=-1)
 
-    mixed, edges = pl.pallas_call(
-        attention_kernel,
+    mixed, top, bottom, sides, corners = pl.pallas_call(
+        functools.partial(attention_kernel, sizes),
         out_shape=(
             jax.ShapeDtypeStruct((height, breadth, width), bf16),
-            jax.ShapeDtypeStruct((2, height * 8, width), bf16),
-        ),
-        in_specs=[SM] + [VM] * 6,
-        out_specs=(VM, VM),
-        scratch_shapes=[
-            pltpu.VMEM((BR + 2, BC + 2, tok, 3 * width), bf16),
-            pltpu.VMEM(((BC + 2) * tok, width), bf16),
-            pltpu.VMEM((BR * BC, tok, width), bf16),
-            pltpu.VMEM((height, breadth, width), f32),
-        ],
-        compiler_params=pltpu.CompilerParams(vmem_limit_bytes=50 * MIB),
-    )(near.astype(jnp.int32), blocks, frame, ln_gain.reshape(1, width), w_qkv, w_out, bias)
-
-    top, bottom, sides, corners = pl.pallas_call(
-        functools.partial(mixed_halo_kernel, sizes),
-        out_shape=(
             jax.ShapeDtypeStruct((3, breadth, width), bf16),
             jax.ShapeDtypeStruct((3, breadth, width), bf16),
             jax.ShapeDtypeStruct((2, height * 8, width), bf16),
             jax.ShapeDtypeStruct((4, 32, width), bf16),
         ),
-        in_specs=[ANY, ANY],
-        out_specs=(ANY,) * 4,
-        scratch_shapes=[dma((8,)), dma((8,))],
-        compiler_params=pltpu.CompilerParams(collective_id=1, has_side_effects=True),
-    )(mixed, edges)
+        in_specs=[SM] + [VM] * 5,
+        out_specs=(VM,) + (ANY,) * 4,
+        scratch_shapes=[
+            pltpu.VMEM((2, height * 8, width), bf16),
+            pltpu.VMEM((BR + 2, BC + 2, tok, width), bf16),
+            pltpu.VMEM((BR + 2, BC + 2, tok, 3 * width), bf16),
+            pltpu.VMEM(((BC + 2) * tok, width), bf16),
+            pltpu.VMEM((BR * BC, tok, width), bf16),
+            pltpu.VMEM((height, breadth, width), f32),
+            dma((8,)),
+            dma((8,)),
+            dma((8,)),
+            dma((8,)),
+        ],
+        compiler_params=pltpu.CompilerParams(
+            vmem_limit_bytes=54 * MIB, collective_id=0, has_side_effects=True
+        ),
+    )(near.astype(jnp.int32), blocks, ln_gain.reshape(1, width), w_qkv, w_out, bias)
 
     flags = jnp.stack([row > 0, row < sizes[0] - 1, col > 0, col < sizes[1] - 1])
     chunks = width // 128

time: 102 us -> 92.5 us (0.907)
  Pallas kernels: 91.5 us -> 79.7 us
  local copies, waits for them, and re-layouts: 9.36 us -> 10.8 us
    pallas_call x3 -> x1, Pallas kernels: 66 us -> 54.2 us  [per_device(): pl.pallas_call(functools.partial(attention_kernel, sizes), out_shape=(jax...]
    unnamed x24 -> x16, local copies, waits for them, and re-layouts: 4.61 us -> 5.39 us
where the time goes in v3:
time: 92.5 us; the launch traced here: 92.1 us
  Pallas kernels  79.7 us (86%)
  local copies, waits for them, and re-layouts  10.8 us (12%)
  other arithmetic  1.58 us (2%)
    pallas_call x1, Pallas kernels, per_device(): pl.pallas_call(functools.partial(attention_kernel, sizes), out_shape=(jax...  54.2 us
    pallas_call x1, Pallas kernels, per_device(): pl.pallas_call(conv_kernel, out_shape=jax.ShapeDtypeStruct((height, bread...  25.5 us
    unnamed x16, local copies, waits for them, and re-layouts  5.39 us
    reshape x1, local copies, waits for them, and re-layouts, per_device(): blocks = tokens.reshape(BR, BLK, BC, BLK, width).transpose(0, 2, 1, 3, 4)  3.2 us

profile of v3, /device:TPU:1, one launch (start us, length us, event | category | flops | bytes accessed | tf_op | source)
XLA Modules:
  0.0 92.1 jit_solution(16323773368138918914)
XLA Ops:
  0.0 0.8 fusion
  0.8 0.1 reshape.87
  0.9 0.1 reshape.88
  1.0 0.7 fusion.1
  1.7 0.1 fusion.2
  1.8 0.1 stack.50
  1.9 0.1 stack.51
  1.9 0.1 stack.52
  2.0 0.1 stack.53
  2.1 0.1 stack.54
  2.2 0.1 stack.55
  2.3 0.1 stack.56
  2.4 0.1 stack.57
  2.5 0.1 stack.58
  2.5 0.1 stack.59
  2.6 0.1 copy.19
  2.7 0.1 broadcast_in_dim.24
  2.8 0.8 broadcast_in_dim.28.bias
  3.6 3.2 %copy.24 = bf16[4,8,8,8,512]{4,3,1,2,0:T(8,128)(2,1)} copy(bf16[4,8,8,8,512]{4,3,2,1,0:T(8,128)(2,1)} %bitcast.22) | data formatting | bytes 4194304 | tf_op jit(solution)/shard_map/reshape | solution.py:360
  6.8 0.0 copy-start.7
  6.8 0.0 copy-start.5
  6.8 0.0 copy-start.6
  6.8 54.2 %shard_map.82 = (bf16[32,64,512]{2,1,0:T(8,128)(2,1)}, bf16[3,64,512]{2,1,0:T(8,128)(2,1)}, bf16[3,64,512]{2,1,0:T(8,128)(2,1)}, bf16[2,256,512]{2,1,0:T(8,128)(2,1)}, bf16[4,32,512]{2,1,0:T(8,128)(2,1)}) custom-call(s32[6,10]{1,0:T(8,128)} %get-tuple-element.15.ok_ref, bf16[4,8,64,512]{3,2,1,0:T(8,128)(2,1)} %bitcast.21, f32[1,512]{1,0:T(1,128)} %bitcast.25, ...), custom_call_target="tpu_custom_call" | custom-call | tf_op jit(solution)/shard_map/pallas_call | solution.py:369
  61.0 0.1 add_convert_fusion.flags
  61.1 0.0 copy-done.7
  61.2 0.1 broadcast_in_dim.27.weight
  61.3 0.0 copy-done.5
  61.3 0.0 copy-done.6
  61.3 0.0 copy-start
  61.3 1.6 %copy-done = bf16[32,64,512]{2,1,0:T(8,128)(2,1)S(1)} copy-done((bf16[32,64,512]{2,1,0:T(8,128)(2,1)S(1)}, bf16[32,64,512]{2,1,0:T(8,128)(2,1)}, u32[]{:S(2)}) %copy-start) | copy-done | bytes 2097176
  62.9 0.0 copy-start.1
  62.9 1.0 %copy-done.1 = bf16[2,256,512]{2,1,0:T(8,128)(2,1)S(1)} copy-done((bf16[2,256,512]{2,1,0:T(8,128)(2,1)S(1)}, bf16[2,256,512]{2,1,0:T(8,128)(2,1)}, u32[]{:S(2)}) %copy-start.1) | copy-done | bytes 524312
  63.9 0.0 copy-start.2
  63.9 0.9 %copy-done.2 = bf16[3,64,512]{2,1,0:T(8,128)(2,1)S(1)} copy-done((bf16[3,64,512]{2,1,0:T(8,128)(2,1)S(1)}, bf16[3,64,512]{2,1,0:T(8,128)(2,1)}, u32[]{:S(2)}) %copy-start.2) | copy-done | bytes 196632
  64.8 0.0 copy-start.3
  64.8 0.9 %copy-done.3 = bf16[3,64,512]{2,1,0:T(8,128)(2,1)S(1)} copy-done((bf16[3,64,512]{2,1,0:T(8,128)(2,1)S(1)}, bf16[3,64,512]{2,1,0:T(8,128)(2,1)}, u32[]{:S(2)}) %copy-start.3) | copy-done | bytes 196632
  65.8 0.0 copy-start.4
  65.8 0.9 copy-done.4
  66.7 25.5 %shard_map.83 = bf16[32,64,512]{2,1,0:T(8,128)(2,1)} custom-call(s32[4]{0:T(128)S(1)} %add_convert_fusion.flags, bf16[32,64,512]{2,1,0:T(8,128)(2,1)S(1)} %copy-done, bf16[3,64,512]{2,1,0:T(8,128)(2,1)S(1)} %copy-done.2, bf16[3,64,512]{2,1,0:T(8,128)(2,1)S(1)} %copy-done.3, bf16[2,256,512]{2,1,0:T(8,128)(2,1)S(1)} %copy-done.1, ...), custom_call_target="tpu_custom_call" | custom-call | tf_op jit(solution)/shard_map/pallas_call | solution.py:401
  (4 shorter events, 0.1 us)
Async XLA Ops:
  6.8 54.3 %copy-start.7 = (f32[7,7,512]{2,1,0:T(8,128)S(1)}, f32[7,7,512]{2,1,0:T(8,128)}, u32[]{:S(2)}) copy-start(f32[7,7,512]{2,1,0:T(8,128)} %param.13) | copy-start | bytes 301060
  6.8 54.4 %copy-start.5 = (f32[512]{0:T(512)S(1)}, f32[512]{0:T(512)}, u32[]{:S(2)}) copy-start(f32[512]{0:T(512)} %param.14) | copy-start | bytes 6148
  6.8 54.5 %copy-start.6 = (f32[512]{0:T(512)S(1)}, f32[512]{0:T(512)}, u32[]{:S(2)}) copy-start(f32[512]{0:T(512)} %param.15) | copy-start | bytes 6148
  61.3 1.6 %copy-start = (bf16[32,64,512]{2,1,0:T(8,128)(2,1)S(1)}, bf16[32,64,512]{2,1,0:T(8,128)(2,1)}, u32[]{:S(2)}) copy-start(bf16[32,64,512]{2,1,0:T(8,128)(2,1)} %get-tuple-element.10.mixed) | copy-start | bytes 6291460
  62.9 1.0 %copy-start.1 = (bf16[2,256,512]{2,1,0:T(8,128)(2,1)S(1)}, bf16[2,256,512]{2,1,0:T(8,128)(2,1)}, u32[]{:S(2)}) copy-start(bf16[2,256,512]{2,1,0:T(8,128)(2,1)} %get-tuple-element.13.sides) | copy-start | bytes 1572868
  63.9 0.9 %copy-start.2 = (bf16[3,64,512]{2,1,0:T(8,128)(2,1)S(1)}, bf16[3,64,512]{2,1,0:T(8,128)(2,1)}, u32[]{:S(2)}) copy-start(bf16[3,64,512]{2,1,0:T(8,128)(2,1)} %get-tuple-element.11.top) | copy-start | bytes 589828
  64.8 0.9 %copy-start.3 = (bf16[3,64,512]{2,1,0:T(8,128)(2,1)S(1)}, bf16[3,64,512]{2,1,0:T(8,128)(2,1)}, u32[]{:S(2)}) copy-start(bf16[3,64,512]{2,1,0:T(8,128)(2,1)} %get-tuple-element.12.bottom) | copy-start | bytes 589828
  65.8 0.9 copy-start.4

commit v4 on v3

--- a/solution.py
+++ b/solution.py
@@ -206,51 +206,52 @@
         == lax.broadcasted_iota(jnp.int32, shape, 1) // head
     )
 
-    def attend(bi, bj):
+    def window(bi, bj, start):
+        return jnp.concatenate(
+            [
+                qkv[bi + a, pl.ds(bj, 3), :, pl.ds(start, half)].reshape(3 * tok, half)
+                for a in range(3)
+            ],
+            axis=0,
+        )
+
+    def score(bi, bj, g):
+        q = qkv[bi + 1, bj + 1, :, pl.ds(g * half, half)].astype(jnp.float32)
+        q = q * head ** (-0.5)
+        q = jnp.where(same, jnp.concatenate([q] * GROUP, axis=0), 0.0)
+        return lax.dot_general(
+            q.astype(jnp.bfloat16),
+            window(bi, bj, width + g * half),
+            (((1,), (1,)), ((), ())),
+            preferred_element_type=jnp.float32,
+        )
+
+    def blend(bi, bj, g, s):
         b = bi * BC + bj
-        ok = ok_ref[bi + 1, bj + 1] != 0
-        for g in range(2):
-            q = qkv[bi + 1, bj + 1, :, pl.ds(g * half, half)].astype(jnp.float32)
-            q = q * head ** (-0.5)
-            q = jnp.where(same, jnp.concatenate([q] * GROUP, axis=0), 0.0)
-            q = q.astype(jnp.bfloat16)
-
-            def window(start):
-                return jnp.concatenate(
-                    [
-                        qkv[bi + a, pl.ds(bj, 3), :, pl.ds(start, half)].reshape(
-                            3 * tok, half
-                        )
-                        for a in range(3)
-                    ],
-                    axis=0,
-                )
-
-            s = lax.dot_general(
-                q,
-                window(width + g * half),
-                (((1,), (1,)), ((), ())),
-                preferred_element_type=jnp.float32,
-            )
-            s = s + bias[b]
-            e = jnp.exp(s - jnp.max(s, axis=-1, keepdims=True))
-            total = jnp.sum(e, axis=-1, keepdims=True)
-            o = jnp.dot(
-                e.astype(jnp.bfloat16),
-                window(2 * width + g * half),
-                preferred_element_type=jnp.float32,
-            )
-            o = jnp.where(same, o * (1.0 / total), 0.0)
-            o = o[:tok] + o[tok : 2 * tok] + o[2 * tok : 3 * tok] + o[3 * tok :]
-            o = jnp.where(ok, o, 0.0)
-            att[b, :, pl.ds(g * half, half)] = o.astype(jnp.bfloat16)
+        s = s + bias[b]
+        e = jnp.exp(s - jnp.max(s, axis=-1, keepdims=True))
+        total = jnp.sum(e, axis=-1, keepdims=True)
+        o = jnp.dot(
+            e.astype(jnp.bfloat16),
+            window(bi, bj, 2 * width + g * half),
+            preferred_element_type=jnp.float32,
+        )
+        o = jnp.where(same, o * (1.0 / total), 0.0)
+        o = o[:tok] + o[tok : 2 * tok] + o[2 * tok : 3 * tok] + o[3 * tok :]
+        o = jnp.where(ok_ref[bi + 1, bj + 1] != 0, o, 0.0)
+        att[b, :, pl.ds(g * half, half)] = o.astype(jnp.bfloat16)
 
     def loop(count, place):
         def step(t, carry):
-            attend(*place(t))
+            jobs = [(*place(2 * t + k), g) for k in range(2) for g in range(2)]
+            s = score(*jobs[0])
+            for n, job in enumerate(jobs):
+                ahead = score(*jobs[n + 1]) if n + 1 < len(jobs) else None
+                blend(*job, s)
+                s = ahead
             return carry
 
-        lax.fori_loop(0, count, step, 0)
+        lax.fori_loop(0, count // 2, step, 0)
 
     def add(places):
         a = jnp.concatenate([att[bi * BC + bj] for bi, bj in places], axis=0)
@@ -335,15 +336,17 @@
 
         lax.fori_loop(0, chunks, lanes, 0)
 
-        def norm(y, inner):
-            f = jnp.concatenate([filt[l, y] for l in range(chunks)], axis=-1)
-            cent = f - jnp.mean(f, axis=-1, keepdims=True)
-            var = jnp.mean(cent * cent, axis=-1, keepdims=True)
-            branch = cent * lax.rsqrt(var + 1e-06) * gain[...]
-            out[r0 + y] = (mixed[r0 + y].astype(f32) + branch).astype(jnp.bfloat16)
+        def norm(t, inner):
+            for y in range(4):
+                y = t * 4 + y
+                f = jnp.concatenate([filt[l, y] for l in range(chunks)], axis=-1)
+                cent = f - jnp.mean(f, axis=-1, keepdims=True)
+                var = jnp.mean(cent * cent, axis=-1, keepdims=True)
+                branch = cent * lax.rsqrt(var + 1e-06) * gain[...]
+                out[r0 + y] = (mixed[r0 + y].astype(f32) + branch).astype(jnp.bfloat16)
             return inner
 
-        lax.fori_loop(0, BLK, norm, 0)
+        lax.fori_loop(0, BLK // 4, norm, 0)
         return carry
 
     lax.fori_loop(0, height // BLK, row_block, 0)
@@ -376,7 +379,7 @@
             jax.ShapeDtypeStruct((4, 32, width), bf16),
         ),
         in_specs=[SM] + [VM] * 5,
-        out_specs=(VM,) + (ANY,) * 4,
+        out_specs=(VM,) * 5,
         scratch_shapes=[
             pltpu.VMEM((2, height * 8, width), bf16),
             pltpu.VMEM((BR + 2, BC + 2, tok, width), bf16),

time: 92.5 us -> 83.5 us (0.903)
  Pallas kernels: 79.7 us -> 70.7 us
    pallas_call x1, Pallas kernels: 54.2 us -> 49.4 us  [per_device(): pl.pallas_call(functools.partial(attention_kernel, sizes), out_shape=(jax...]
    pallas_call x1, Pallas kernels: 25.5 us -> 21.3 us  [per_device(): pl.pallas_call(conv_kernel, out_shape=jax.ShapeDtypeStruct((height, bread...]
where the time goes in v4:
time: 83.5 us; the launch traced here: 83.2 us
  Pallas kernels  70.7 us (85%)
  local copies, waits for them, and re-layouts  10.8 us (13%)
  other arithmetic  1.58 us (2%)
    pallas_call x1, Pallas kernels, per_device(): pl.pallas_call(functools.partial(attention_kernel, sizes), out_shape=(jax...  49.4 us
    pallas_call x1, Pallas kernels, per_device(): pl.pallas_call(conv_kernel, out_shape=jax.ShapeDtypeStruct((height, bread...  21.3 us
    unnamed x16, local copies, waits for them, and re-layouts  5.39 us
    reshape x1, local copies, waits for them, and re-layouts, per_device(): blocks = tokens.reshape(BR, BLK, BC, BLK, width).transpose(0, 2, 1, 3, 4)  3.2 us

profile of v4, /device:TPU:1, one launch (start us, length us, event | category | flops | bytes accessed | tf_op | source)
XLA Modules:
  0.0 83.2 jit_solution(1524612910187095828)
XLA Ops:
  0.0 0.8 %fusion = pred[4,4,32]{2,1,0:T(4,128)(4,1)S(1)} fusion(s32[4,4,24]{2,1,0:T(4,128)} %param.9), kind=kLoop, calls=%fused_computation.2 | loop fusion | flops 24064 | bytes 2048 | tf_op jit(solution)/shard_map/reduce_or | solution.py:24
  0.8 0.1 reshape.87
  0.9 0.1 reshape.88
  1.0 0.7 fusion.1
  1.7 0.1 fusion.2
  1.8 0.1 stack.50
  1.9 0.1 stack.51
  1.9 0.1 stack.52
  2.0 0.1 stack.53
  2.1 0.1 stack.54
  2.2 0.1 stack.55
  2.3 0.1 stack.56
  2.4 0.1 stack.57
  2.5 0.1 stack.58
  2.5 0.1 stack.59
  2.6 0.1 copy.19
  2.7 0.1 broadcast_in_dim.24
  2.8 0.8 broadcast_in_dim.28.bias
  3.6 3.2 %copy.24 = bf16[4,8,8,8,512]{4,3,1,2,0:T(8,128)(2,1)} copy(bf16[4,8,8,8,512]{4,3,2,1,0:T(8,128)(2,1)} %bitcast.22) | data formatting | bytes 4194304 | tf_op jit(solution)/shard_map/reshape | solution.py:363
  6.8 0.0 copy-start.7
  6.8 0.0 copy-start.5
  6.8 0.0 copy-start.6
  6.8 49.4 %shard_map.82 = (bf16[32,64,512]{2,1,0:T(8,128)(2,1)}, bf16[3,64,512]{2,1,0:T(8,128)(2,1)}, bf16[3,64,512]{2,1,0:T(8,128)(2,1)}, bf16[2,256,512]{2,1,0:T(8,128)(2,1)}, bf16[4,32,512]{2,1,0:T(8,128)(2,1)}) custom-call(s32[6,10]{1,0:T(8,128)} %get-tuple-element.15.ok_ref, bf16[4,8,64,512]{3,2,1,0:T(8,128)(2,1)} %bitcast.21, f32[1,512]{1,0:T(1,128)} %bitcast.25, ...), custom_call_target="tpu_custom_call" | custom-call | tf_op jit(solution)/shard_map/pallas_call | solution.py:372
  56.2 0.1 add_convert_fusion.flags
  56.3 0.0 copy-done.7
  56.4 0.1 broadcast_in_dim.27.weight
  56.4 0.0 copy-done.5
  56.4 0.0 copy-done.6
  56.4 0.0 copy-start
  56.5 1.6 %copy-done = bf16[32,64,512]{2,1,0:T(8,128)(2,1)S(1)} copy-done((bf16[32,64,512]{2,1,0:T(8,128)(2,1)S(1)}, bf16[32,64,512]{2,1,0:T(8,128)(2,1)}, u32[]{:S(2)}) %copy-start) | copy-done | bytes 2097176
  58.0 0.0 copy-start.1
  58.0 1.0 %copy-done.1 = bf16[2,256,512]{2,1,0:T(8,128)(2,1)S(1)} copy-done((bf16[2,256,512]{2,1,0:T(8,128)(2,1)S(1)}, bf16[2,256,512]{2,1,0:T(8,128)(2,1)}, u32[]{:S(2)}) %copy-start.1) | copy-done | bytes 524312
  59.1 0.0 copy-start.2
  59.1 0.9 %copy-done.2 = bf16[3,64,512]{2,1,0:T(8,128)(2,1)S(1)} copy-done((bf16[3,64,512]{2,1,0:T(8,128)(2,1)S(1)}, bf16[3,64,512]{2,1,0:T(8,128)(2,1)}, u32[]{:S(2)}) %copy-start.2) | copy-done | bytes 196632
  60.0 0.0 copy-start.3
  60.0 0.9 %copy-done.3 = bf16[3,64,512]{2,1,0:T(8,128)(2,1)S(1)} copy-done((bf16[3,64,512]{2,1,0:T(8,128)(2,1)S(1)}, bf16[3,64,512]{2,1,0:T(8,128)(2,1)}, u32[]{:S(2)}) %copy-start.3) | copy-done | bytes 196632
  60.9 0.0 copy-start.4
  60.9 0.9 %copy-done.4 = bf16[4,32,512]{2,1,0:T(8,128)(2,1)S(1)} copy-done((bf16[4,32,512]{2,1,0:T(8,128)(2,1)S(1)}, bf16[4,32,512]{2,1,0:T(8,128)(2,1)}, u32[]{:S(2)}) %copy-start.4) | copy-done | bytes 131096
  61.8 21.3 %shard_map.83 = bf16[32,64,512]{2,1,0:T(8,128)(2,1)} custom-call(s32[4]{0:T(128)S(1)} %add_convert_fusion.flags, bf16[32,64,512]{2,1,0:T(8,128)(2,1)S(1)} %copy-done, bf16[3,64,512]{2,1,0:T(8,128)(2,1)S(1)} %copy-done.2, bf16[3,64,512]{2,1,0:T(8,128)(2,1)S(1)} %copy-done.3, bf16[2,256,512]{2,1,0:T(8,128)(2,1)S(1)} %copy-done.1, ...), custom_call_target="tpu_custom_call" | custom-call | tf_op jit(solution)/shard_map/pallas_call | solution.py:404
  (4 shorter events, 0.1 us)
Async XLA Ops:
  6.8 49.5 %copy-start.7 = (f32[7,7,512]{2,1,0:T(8,128)S(1)}, f32[7,7,512]{2,1,0:T(8,128)}, u32[]{:S(2)}) copy-start(f32[7,7,512]{2,1,0:T(8,128)} %param.13) | copy-start | bytes 301060
  6.8 49.6 %copy-start.5 = (f32[512]{0:T(512)S(1)}, f32[512]{0:T(512)}, u32[]{:S(2)}) copy-start(f32[512]{0:T(512)} %param.14) | copy-start | bytes 6148
  6.8 49.6 %copy-start.6 = (f32[512]{0:T(512)S(1)}, f32[512]{0:T(512)}, u32[]{:S(2)}) copy-start(f32[512]{0:T(512)} %param.15) | copy-start | bytes 6148
  56.4 1.6 %copy-start = (bf16[32,64,512]{2,1,0:T(8,128)(2,1)S(1)}, bf16[32,64,512]{2,1,0:T(8,128)(2,1)}, u32[]{:S(2)}) copy-start(bf16[32,64,512]{2,1,0:T(8,128)(2,1)} %get-tuple-element.10.mixed) | copy-start | bytes 6291460
  58.0 1.0 %copy-start.1 = (bf16[2,256,512]{2,1,0:T(8,128)(2,1)S(1)}, bf16[2,256,512]{2,1,0:T(8,128)(2,1)}, u32[]{:S(2)}) copy-start(bf16[2,256,512]{2,1,0:T(8,128)(2,1)} %get-tuple-element.13.sides) | copy-start | bytes 1572868
  59.1 0.9 %copy-start.2 = (bf16[3,64,512]{2,1,0:T(8,128)(2,1)S(1)}, bf16[3,64,512]{2,1,0:T(8,128)(2,1)}, u32[]{:S(2)}) copy-start(bf16[3,64,512]{2,1,0:T(8,128)(2,1)} %get-tuple-element.11.top) | copy-start | bytes 589828
  60.0 0.9 %copy-start.3 = (bf16[3,64,512]{2,1,0:T(8,128)(2,1)S(1)}, bf16[3,64,512]{2,1,0:T(8,128)(2,1)}, u32[]{:S(2)}) copy-start(bf16[3,64,512]{2,1,0:T(8,128)(2,1)} %get-tuple-element.12.bottom) | copy-start | bytes 589828
  60.9 0.9 %copy-start.4 = (bf16[4,32,512]{2,1,0:T(8,128)(2,1)S(1)}, bf16[4,32,512]{2,1,0:T(8,128)(2,1)}, u32[]{:S(2)}) copy-start(bf16[4,32,512]{2,1,0:T(8,128)(2,1)} %get-tuple-element.14.corners) | copy-start | bytes 393220

commit v5 on v4

--- a/solution.py
+++ b/solution.py
@@ -124,7 +124,7 @@
 def attention_kernel(
     sizes,
     ok_ref,
-    blocks,
+    tokens,
     gain,
     w_qkv,
     w_out,
@@ -135,6 +135,7 @@
     sides,
     corners,
     edges,
+    blocks,
     frame,
     qkv,
     normed,
@@ -145,6 +146,16 @@
     send_b,
     recv_b,
 ):
+    def cut(bi, carry):
+        for pair in range(BC // 2):
+            x = tokens[pl.ds(bi * BLK, BLK), pl.ds(pair * 2 * BLK, 2 * BLK), :]
+            x = x.astype(jnp.float32).reshape(BLK, 2, BLK, x.shape[-1])
+            for k in range(2):
+                part = x[:, k].reshape(BLK * BLK, x.shape[-1])
+                blocks[bi, 2 * pair + k] = part.astype(jnp.bfloat16)
+        return carry
+
+    lax.fori_loop(0, BR, cut, 0)
     landed = exchange(sizes, token_views(blocks, frame), send_a, recv_a, True)
     width = frame.shape[-1]
     tok = BLK * BLK
@@ -360,8 +371,6 @@
     row, col = lax.axis_index("row"), lax.axis_index("col")
     dma = pltpu.SemaphoreType.DMA
 
-    blocks = tokens.reshape(BR, BLK, BC, BLK, width).transpose(0, 2, 1, 3, 4)
-    blocks = blocks.reshape(BR, BC, tok, width)
     table = jnp.pad(block_table(tissue_list), 1)
     near = lax.dynamic_slice(table, (row * BR, col * BC), (BR + 2, BC + 2))
     okay = jnp.stack(
@@ -382,6 +391,7 @@
         out_specs=(VM,) * 5,
         scratch_shapes=[
             pltpu.VMEM((2, height * 8, width), bf16),
+            pltpu.VMEM((BR, BC, tok, width), bf16),
             pltpu.VMEM((BR + 2, BC + 2, tok, width), bf16),
             pltpu.VMEM((BR + 2, BC + 2, tok, 3 * width), bf16),
             pltpu.VMEM(((BC + 2) * tok, width), bf16),
@@ -395,7 +405,7 @@
         compiler_params=pltpu.CompilerParams(
             vmem_limit_bytes=54 * MIB, collective_id=0, has_side_effects=True
         ),
-    )(near.astype(jnp.int32), blocks, ln_gain.reshape(1, width), w_qkv, w_out, bias)
+    )(near.astype(jnp.int32), tokens, ln_gain.reshape(1, width), w_qkv, w_out, bias)
 
     flags = jnp.stack([row > 0, row < sizes[0] - 1, col > 0, col < sizes[1] - 1])
     chunks = width // 128

time: 83.5 us -> 81.4 us (0.975)
  local copies, waits for them, and re-layouts: 10.8 us -> 8.48 us
    reshape x1 -> x0, local copies, waits for them, and re-layouts: 3.2 us -> none  [per_device(): blocks = tokens.reshape(BR, BLK, BC, BLK, width).transpose(0, 2, 1, 3, 4)]
    reshape x2, local copies, waits for them, and re-layouts: 0.05 us -> 0.95 us  [per_device(): weight = conv_weight.reshape(49, chunks, 1, 128).transpose(1, 0, 2, 3)]
    unnamed x16 -> x14, local copies, waits for them, and re-layouts: 5.39 us -> 5.39 us
where the time goes in v5:
time: 81.4 us; the launch traced here: 81 us
  Pallas kernels  70.9 us (87%)
  local copies, waits for them, and re-layouts  8.48 us (10%)
  other arithmetic  1.59 us (2%)
    pallas_call x1, Pallas kernels, per_device(): pl.pallas_call(functools.partial(attention_kernel, sizes), out_shape=(jax...  49.5 us
    pallas_call x1, Pallas kernels, per_device(): pl.pallas_call(conv_kernel, out_shape=jax.ShapeDtypeStruct((height, bread...  21.3 us
    unnamed x14, local copies, waits for them, and re-layouts  5.39 us

profile of v5, /device:TPU:1, one launch (start us, length us, event | category | flops | bytes accessed | tf_op | source)
XLA Modules:
  0.0 81.0 jit_solution(6034603076557634111)
XLA Ops:
  0.0 0.1 add_convert_fusion.flags
  0.1 0.8 %fusion = pred[4,4,32]{2,1,0:T(4,128)(4,1)S(1)} fusion(s32[4,4,24]{2,1,0:T(4,128)} %param.9), kind=kLoop, calls=%fused_computation.1 | loop fusion | flops 24064 | bytes 2048 | tf_op jit(solution)/shard_map/reduce_or | solution.py:24
  0.9 0.1 reshape.81
  1.0 0.1 reshape.82
  1.1 0.7 fusion.1
  1.8 0.1 fusion.2
  1.9 0.1 stack.58
  1.9 0.1 stack.57
  2.0 0.1 stack.56
  2.1 0.1 stack.55
  2.2 0.1 stack.54
  2.3 0.1 stack.53
  2.4 0.1 stack.52
  2.5 0.1 stack.51
  2.5 0.1 stack.50
  2.6 0.1 stack.59
  2.7 0.1 copy.16
  2.8 0.9 %reshape.84 = f32[49,4,1,128]{3,1,0,2:T(4,128)S(1)} reshape(f32[7,7,512]{2,1,0:T(8,128)} %param.13) | data formatting | bytes 200704 | tf_op jit(solution)/shard_map/reshape | solution.py:412
  3.8 0.1 broadcast_in_dim.24
  3.9 0.8 broadcast_in_dim.28.bias
  4.7 0.1 broadcast_in_dim.27.weight
  4.7 0.0 copy-start.5
  4.7 0.0 copy-start.6
  4.7 49.5 %shard_map.82 = (bf16[32,64,512]{2,1,0:T(8,128)(2,1)}, bf16[3,64,512]{2,1,0:T(8,128)(2,1)}, bf16[3,64,512]{2,1,0:T(8,128)(2,1)}, bf16[2,256,512]{2,1,0:T(8,128)(2,1)}, bf16[4,32,512]{2,1,0:T(8,128)(2,1)}) custom-call(s32[6,10]{1,0:T(8,128)} %get-tuple-element.15.ok_ref, bf16[32,64,512]{2,1,0:T(8,128)(2,1)} %tokens.1, f32[1,512]{1,0:T(1,128)} %bitcast.17, ...), custom_call_target="tpu_custom_call" | custom-call | tf_op jit(solution)/shard_map/pallas_call | solution.py:381
  54.3 0.0 copy-done.5
  54.3 0.0 copy-done.6
  54.3 0.0 copy-start
  54.3 1.6 %copy-done = bf16[32,64,512]{2,1,0:T(8,128)(2,1)S(1)} copy-done((bf16[32,64,512]{2,1,0:T(8,128)(2,1)S(1)}, bf16[32,64,512]{2,1,0:T(8,128)(2,1)}, u32[]{:S(2)}) %copy-start) | copy-done | bytes 2097176
  55.9 0.0 copy-start.1
  55.9 1.0 %copy-done.1 = bf16[2,256,512]{2,1,0:T(8,128)(2,1)S(1)} copy-done((bf16[2,256,512]{2,1,0:T(8,128)(2,1)S(1)}, bf16[2,256,512]{2,1,0:T(8,128)(2,1)}, u32[]{:S(2)}) %copy-start.1) | copy-done | bytes 524312
  56.9 0.0 copy-start.2
  56.9 0.9 %copy-done.2 = bf16[3,64,512]{2,1,0:T(8,128)(2,1)S(1)} copy-done((bf16[3,64,512]{2,1,0:T(8,128)(2,1)S(1)}, bf16[3,64,512]{2,1,0:T(8,128)(2,1)}, u32[]{:S(2)}) %copy-start.2) | copy-done | bytes 196632
  57.9 0.0 copy-start.3
  57.9 0.9 %copy-done.3 = bf16[3,64,512]{2,1,0:T(8,128)(2,1)S(1)} copy-done((bf16[3,64,512]{2,1,0:T(8,128)(2,1)S(1)}, bf16[3,64,512]{2,1,0:T(8,128)(2,1)}, u32[]{:S(2)}) %copy-start.3) | copy-done | bytes 196632
  58.8 0.0 copy-start.4
  58.8 0.9 %copy-done.4 = bf16[4,32,512]{2,1,0:T(8,128)(2,1)S(1)} copy-done((bf16[4,32,512]{2,1,0:T(8,128)(2,1)S(1)}, bf16[4,32,512]{2,1,0:T(8,128)(2,1)}, u32[]{:S(2)}) %copy-start.4) | copy-done | bytes 131096
  59.7 21.3 %shard_map.83 = bf16[32,64,512]{2,1,0:T(8,128)(2,1)} custom-call(s32[4]{0:T(128)S(1)} %add_convert_fusion.flags, bf16[32,64,512]{2,1,0:T(8,128)(2,1)S(1)} %copy-done, bf16[3,64,512]{2,1,0:T(8,128)(2,1)S(1)} %copy-done.2, bf16[3,64,512]{2,1,0:T(8,128)(2,1)S(1)} %copy-done.3, bf16[2,256,512]{2,1,0:T(8,128)(2,1)S(1)} %copy-done.1, ...), custom_call_target="tpu_custom_call" | custom-call | tf_op jit(solution)/shard_map/pallas_call | solution.py:414
  (3 shorter events, 0.0 us)
Async XLA Ops:
  4.7 49.6 %copy-start.5 = (f32[512]{0:T(512)S(1)}, f32[512]{0:T(512)}, u32[]{:S(2)}) copy-start(f32[512]{0:T(512)} %param.14) | copy-start | bytes 6148
  4.7 49.6 %copy-start.6 = (f32[512]{0:T(512)S(1)}, f32[512]{0:T(512)}, u32[]{:S(2)}) copy-start(f32[512]{0:T(512)} %param.15) | copy-start | bytes 6148
  54.3 1.6 %copy-start = (bf16[32,64,512]{2,1,0:T(8,128)(2,1)S(1)}, bf16[32,64,512]{2,1,0:T(8,128)(2,1)}, u32[]{:S(2)}) copy-start(bf16[32,64,512]{2,1,0:T(8,128)(2,1)} %get-tuple-element.10.mixed) | copy-start | bytes 6291460
  55.9 1.0 %copy-start.1 = (bf16[2,256,512]{2,1,0:T(8,128)(2,1)S(1)}, bf16[2,256,512]{2,1,0:T(8,128)(2,1)}, u32[]{:S(2)}) copy-start(bf16[2,256,512]{2,1,0:T(8,128)(2,1)} %get-tuple-element.13.sides) | copy-start | bytes 1572868
  56.9 0.9 %copy-start.2 = (bf16[3,64,512]{2,1,0:T(8,128)(2,1)S(1)}, bf16[3,64,512]{2,1,0:T(8,128)(2,1)}, u32[]{:S(2)}) copy-start(bf16[3,64,512]{2,1,0:T(8,128)(2,1)} %get-tuple-element.11.top) | copy-start | bytes 589828
  57.9 0.9 %copy-start.3 = (bf16[3,64,512]{2,1,0:T(8,128)(2,1)S(1)}, bf16[3,64,512]{2,1,0:T(8,128)(2,1)}, u32[]{:S(2)}) copy-start(bf16[3,64,512]{2,1,0:T(8,128)(2,1)} %get-tuple-element.12.bottom) | copy-start | bytes 589828
  58.8 0.9 %copy-start.4 = (bf16[4,32,512]{2,1,0:T(8,128)(2,1)S(1)}, bf16[4,32,512]{2,1,0:T(8,128)(2,1)}, u32[]{:S(2)}) copy-start(bf16[4,32,512]{2,1,0:T(8,128)(2,1)} %get-tuple-element.14.corners) | copy-start | bytes 393220
